TPU v7x, 128 devices: a whole 4x4x4 slice. The times are simulated.
128 devices in a mesh: traj: 16 (over y, x), tensor: 8 (over z, core).
Axes of the slice: x: 4, y: 4, z: 4, core: 2. Of those that a mesh axis runs over, the one named last changes fastest.
Arguments:
- ssm_in: bfloat16 [16, 256, 8192], P('traj', None, 'tensor'), may hold values from -6 to 6
- gate_in: bfloat16 [16, 256, 8192], P('traj', None, 'tensor'), may hold values from -6 to 6
- b_in: bfloat16 [16, 256, 2048], P('traj', None, 'tensor'), may hold values from -1.5 to 1.5
- c_in: bfloat16 [16, 256, 2048], P('traj', None, 'tensor'), may hold values from -1.5 to 1.5
- dt_in: float32 [16, 256, 128], P('traj', None, 'tensor'), may hold values from -5 to 5
- dt_bias: float32 [128], P('tensor'), may hold values from -2 to 0
- decay_rate: float32 [128], P('tensor'), may hold values from 0.005 to 0.25
- skip: float32 [128], P('tensor'), may hold values from 0.5 to 1.5
- norm_gain: float32 [8192], P('tensor'), may hold values from 0.5 to 1.5
- out_weight: bfloat16 [8192, 8192], P('tensor'), may hold values from -0.09375 to 0.09375
- state_roll: float32 [16, 128, 64, 256], P(None, 'tensor', 'traj'), may hold values from -4 to 4
- query: bfloat16 [16, 256, 8192], P('traj', None, 'tensor'), may hold values from -6 to 6
- new_kv: bfloat16 [2, 16, 256, 1024], P(None, 'traj', None, 'tensor'), may hold values from -6 to 6
- prefix_kv: bfloat16 [2, 16, 8192, 1024], P(None, None, ('traj', 'tensor')), may hold values from -6 to 6
- prefix_len: int32 [16], replicated, may hold values from 1024 to 8192, as said below
- order: int32 [16], replicated, may hold values from 0 to 15, each once
Outputs:
- mixed: bfloat16 [16, 256, 8192], P('traj', None, 'tensor')
- final_state: float32 [16, 128, 64, 256], P('traj', 'tensor')
- attended: bfloat16 [16, 256, 8192], P('traj', None, 'tensor')
Inputs may be any that keep to these rules, and one draw needn't show every extreme that they name: `prefix_len`: some trajectory has exactly 8192 prefix positions. `order`: each rollout trajectory is taken by exactly one slot.
All inputs are finite; a program needn't handle non-finite values.
Results may differ from a plain program's by a relative error of at most 0.02.
Values may be sent and summed in bfloat16 or wider, within the bound.
No kernel may reach another device: no remote copies, remote signals or barrier semaphores. Data moves between devices by JAX's collectives and lax.ppermute only.
A program may use at most 128 MiB of HBM per device.

v0:
```python
import math

import jax
import jax.numpy as jnp
from jax import lax
from jax.sharding import PartitionSpec as P

HEAD_DIM = 64
STATE = 256
ATT_DIM = 128


def mixer_core(
    ssm_x, gate_z, b_rows, c_rows, dt_raw, start_state, dt_bias, decay_rate, skip, norm_gain
):
    seg = ssm_x.shape[0]
    heads = dt_raw.shape[1]
    groups = b_rows.shape[1] // STATE
    per_group = heads // groups
    step = jax.nn.softplus(dt_raw + dt_bias[None, :])
    cum = jnp.cumsum(-step * decay_rate[None, :], axis=0)
    rows_idx = lax.broadcasted_iota(jnp.int32, (seg, seg), 0)
    cols_idx = lax.broadcasted_iota(jnp.int32, (seg, seg), 1)
    causal = rows_idx >= cols_idx
    diff = cum[:, None, :] - cum[None, :, :]
    decay_mat = jnp.exp(jnp.where(causal[:, :, None], diff, -jnp.inf))
    x_heads = ssm_x.astype(jnp.float32).reshape(seg, heads, HEAD_DIM)
    b_plain = b_rows.reshape(seg, groups, STATE)
    c_plain = c_rows.reshape(seg, groups, STATE)
    b_group = b_plain.astype(jnp.float32)
    c_group = c_plain.astype(jnp.float32)
    b_heads = jnp.repeat(b_group, per_group, axis=1)
    c_heads = jnp.repeat(c_group, per_group, axis=1)
    inner = jnp.einsum("tgn,jgn->gtj", c_plain, b_plain, preferred_element_type=jnp.float32)
    inner_heads = jnp.repeat(inner, per_group, axis=0)
    mixing = jnp.transpose(decay_mat, (2, 0, 1)) * inner_heads * jnp.transpose(step)[:, None, :]
    out_y = jnp.einsum("htj,jhp->thp", mixing, x_heads, precision=lax.Precision.HIGHEST)
    carried = jnp.einsum("thn,hpn->thp", c_heads, start_state, precision=lax.Precision.HIGHEST)
    out_y = out_y + jnp.exp(cum)[:, :, None] * carried
    out_y = out_y + skip[None, :, None] * x_heads
    tail = jnp.exp(cum[-1][None, :] - cum) * step
    final = jnp.exp(cum[-1])[:, None, None] * start_state + jnp.einsum(
        "jh,jhp,jhn->hpn", tail, x_heads, b_heads, precision=lax.Precision.HIGHEST
    )
    gated = out_y.reshape(seg, -1) * jax.nn.silu(gate_z.astype(jnp.float32))
    grouped = gated.reshape(seg, groups, -1)
    factor = lax.rsqrt(jnp.mean(grouped * grouped, axis=-1, keepdims=True) + 1e-05)
    normed = ((grouped * factor).reshape(seg, -1) * norm_gain[None, :]).astype(jnp.bfloat16)
    return (normed, final)


def attend(queries, keys, values, length, npre):
    seg = queries.shape[0]
    nkeys = keys.shape[0]
    qheads = queries.shape[1] // ATT_DIM
    kvheads = keys.shape[1] // ATT_DIM
    ratio = qheads // kvheads
    q_heads = jnp.transpose(queries.reshape(seg, qheads, ATT_DIM), (1, 0, 2))
    key_heads = keys.reshape(nkeys, kvheads, ATT_DIM)
    value_heads = values.reshape(nkeys, kvheads, ATT_DIM)
    kpos = lax.broadcasted_iota(jnp.int32, (seg, nkeys), 1)
    tpos = lax.broadcasted_iota(jnp.int32, (seg, nkeys), 0)
    valid = jnp.where(kpos < npre, kpos < length, kpos - npre <= tpos)
    factor = 1.0 / math.sqrt(ATT_DIM)

    def one_head(item):
        q_one, head = item
        kv_head = head // ratio
        k_one = lax.dynamic_index_in_dim(key_heads, kv_head, 1, keepdims=False)
        v_one = lax.dynamic_index_in_dim(value_heads, kv_head, 1, keepdims=False)
        score = (
            lax.dot_general(
                q_one, k_one, (((1,), (1,)), ((), ())), preferred_element_type=jnp.float32
            )
            * factor
        )
        score = jnp.where(valid, score, -jnp.inf)
        top = jnp.max(score, axis=1, keepdims=True)
        expo = jnp.exp(score - top)
        total = jnp.sum(expo, axis=1, keepdims=True)
        summed = jnp.dot(expo.astype(jnp.bfloat16), v_one, preferred_element_type=jnp.float32)
        return (summed / total).astype(jnp.bfloat16)

    result = lax.map(one_head, (q_heads, jnp.arange(qheads, dtype=jnp.int32)))
    return jnp.transpose(result, (1, 0, 2)).reshape(seg, -1)


def local(
    ssm_in,
    gate_in,
    b_in,
    c_in,
    dt_in,
    dt_bias,
    decay_rate,
    skip,
    norm_gain,
    out_weight,
    state_roll,
    query,
    new_kv,
    prefix_kv,
    prefix_len,
    order,
):
    slot = lax.axis_index("traj")
    taken = lax.dynamic_index_in_dim(order, slot, 0, keepdims=False)
    length = lax.dynamic_index_in_dim(prefix_len, taken, 0, keepdims=False)
    own_state = lax.all_to_all(
        state_roll[order].astype(jnp.bfloat16), "traj", split_axis=0, concat_axis=2, tiled=True
    ).astype(jnp.float32)
    pfx = prefix_kv.shape[2]
    columns = prefix_kv.shape[3]
    tensor_count = lax.axis_size("tensor")
    width = columns // tensor_count
    slots = prefix_kv.shape[1]
    arranged = prefix_kv.reshape(2, slots, pfx, tensor_count, width)[:, order]
    arranged = jnp.transpose(arranged, (0, 2, 1, 3, 4)).reshape(2, pfx, slots * tensor_count, width)
    received = lax.all_to_all(arranged, ("traj", "tensor"), split_axis=2, concat_axis=1, tiled=True)
    own_kv = received.reshape(2, 1, -1, width)
    normed, final = mixer_core(
        ssm_in[0],
        gate_in[0],
        b_in[0],
        c_in[0],
        dt_in[0],
        own_state[0],
        dt_bias,
        decay_rate,
        skip,
        norm_gain,
    )
    partial_out = jnp.dot(normed, out_weight, preferred_element_type=jnp.float32)[None]
    mixed = lax.psum_scatter(
        partial_out.astype(jnp.bfloat16), "tensor", scatter_dimension=2, tiled=True
    )
    keys = jnp.concatenate([own_kv[0, 0], new_kv[0, 0]], axis=0)
    values = jnp.concatenate([own_kv[1, 0], new_kv[1, 0]], axis=0)
    attended = attend(query[0], keys, values, length, own_kv.shape[2])
    return (mixed, final[None], attended[None])


def solution(mesh):
    in_specs = (
        P("traj", None, "tensor"),
        P("traj", None, "tensor"),
        P("traj", None, "tensor"),
        P("traj", None, "tensor"),
        P("traj", None, "tensor"),
        P("tensor"),
        P("tensor"),
        P("tensor"),
        P("tensor"),
        P("tensor", None),
        P(None, "tensor", "traj", None),
        P("traj", None, "tensor"),
        P(None, "traj", None, "tensor"),
        P(None, None, ("traj", "tensor"), None),
        P(),
        P(),
    )
    out_specs = (
        P("traj", None, "tensor"),
        P("traj", "tensor", None, None),
        P("traj", None, "tensor"),
    )
    return jax.shard_map(local, mesh=mesh, in_specs=in_specs, out_specs=out_specs, check_vma=False)
```

profile of v0, /device:TPU:1, one launch (start us, length us, event | category | flops | bytes accessed | tf_op | source)
XLA Modules:
  0.0 195.1 jit_solution(5688047439318391730)
XLA Ops:
  10.3 7.6 %all-to-all-start = ((bf16[16,16,4,256]{3,2,1,0:T(4,128)(2,1)}), bf16[16,16,4,256]{3,2,1,0:T(4,128)(2,1)S(1)}, u32[]{:S(2)}, u32[]{:S(2)}) async-start(bf16[16,16,4,256]{3,2,1,0:T(4,128)(2,1)} %gather_fusion), calls=%async_computation | async-start | bytes 1048576 | tf_op jit(solution)/shard_map/all_to_all | solution.py:109
  24.3 5.3 %copy.68 = bf16[256,8,8,128]{3,2,1,0:T(8,128)(2,1)} copy(bf16[256,8,8,128]{3,1,2,0:T(8,128)(2,1)} %bitcast.152) | data formatting | bytes 8388608
  29.6 5.2 %gather_fusion.1 = bf16[16,2,64,8,128]{4,3,2,1,0:T(8,128)(2,1)} fusion(bf16[2,16,64,8,128]{4,3,2,1,0:T(8,128)(2,1)} %bitcast.149, s32[1024]{0:T(1024)S(1)} %pad_clamp_fusion), kind=kCustom, calls=%fused_computation.1 | custom fusion | bytes 8388672 | tf_op jit(solution)/shard_map/gather | solution.py:117
  34.8 5.5 %copy_bitcast_fusion = bf16[2,64,128,128]{3,2,1,0:T(8,128)(2,1)} fusion(bf16[16,2,64,8,128]{4,3,2,1,0:T(8,128)(2,1)} %gather_fusion.1), kind=kLoop, calls=%fused_computation.23 | loop fusion | bytes 8388608 | tf_op jit(solution)/shard_map/reshape | solution.py:118
  41.1 6.9 %copy.62 = bf16[2,64,128,128]{3,1,0,2:T(8,128)(2,1)} copy(bf16[2,64,128,128]{3,2,1,0:T(8,128)(2,1)} %copy_bitcast_fusion) | data formatting | bytes 8388608 | tf_op jit(solution)/shard_map/reshape | solution.py:118
  49.4 11.6 %all-to-all-start.1 = ((bf16[2,64,128,128]{3,1,0,2:T(8,128)(2,1)}), bf16[2,64,128,128]{3,1,0,2:T(8,128)(2,1)}, u32[]{:S(2)}, u32[]{:S(2)}) async-start(bf16[2,64,128,128]{3,1,0,2:T(8,128)(2,1)} %copy.62), calls=%async_computation.2 | async-start | bytes 8388608 | tf_op jit(solution)/shard_map/all_to_all | solution.py:119
  67.5 5.1 %fusion.63 = f32[256,16,64]{0,2,1:T(8,128)} fusion(bf16[256,16,64]{0,2,1:T(8,128)(2,1)S(1)} %bitcast.154, f32[16,256]{1,0:T(8,128)S(1)} %get-tuple-element.128, f32[256,256]{1,0:T(8,128)S(1)} %fusion.85, f32[16,256]{1,0:T(8,128)} %get-tuple-element.131, pred[256,256]{1,0:T(8,128)(4,1)} %iota_compare_fusion.1), kind=kOutput, calls=%fused_computation.46 | convolution fusion | flops 809500672 | bytes 1933312 | tf_op jit(solution)/shard_map/htj,jhp->thp/dot_general | solution.py:37
  73.0 4.3 %multiply_reduce_fusion = (f32[256]{0:T(256)S(1)}, f32[256,16,64]{0,2,1:T(8,128)}) fusion(f32[256,16,64]{0,2,1:T(8,128)S(1)} %bitcast.157, bf16[256,16,64]{0,2,1:T(8,128)(2,1)S(1)} %bitcast.155, f32[16]{0:T(128)S(1)} %copy-done.18, f32[256,16,64]{0,2,1:T(8,128)} %fusion.63, bf16[16,64,256]{2,1,0:T(8,128)(2,1)S(1)} %squeeze.47, ...), kind=kOutput, calls=%fused_computation.59 | convolution fusion | flops 808451840 | bytes 4473920 | tf_op jit(solution)/shard_map/thn,hpn->thp/dot_general | solution.py:38
  78.9 12.2 %fusion.34 = bf16[1,256,8192]{2,1,0:T(8,128)(2,1)} fusion(bf16[1024,8192]{1,0:T(8,128)(2,1)} %param.27, f32[256,1024]{1,0:T(8,128)S(1)} %copy.58, f32[1024]{0:T(1024)S(1)} %copy-done.17, f32[256]{0:T(256)S(1)} %add_rsqrt_fusion, bf16[1,256,1024]{2,1,0:T(8,128)(2,1)S(1)} %copy-done.2), kind=kOutput, calls=%fused_computation.22 | convolution fusion | flops 4299423744 | bytes 22549504 | tf_op jit(solution)/shard_map/dot_general | solution.py:133
  91.7 3.3 %fusion.69 = f32[1,16,64,256]{3,2,1,0:T(8,128)} fusion(f32[256,256]{1,0:T(8,128)S(1)} %bitcast_convert_fusion, bf16[256,16,64]{0,2,1:T(8,128)(2,1)S(1)} %bitcast.156, bf16[16,64,256]{2,1,0:T(8,128)(2,1)S(1)} %squeeze.47, f32[256,16]{0,1:T(8,128)S(1)} %get-tuple-element.127, f32[16]{0:T(128)S(1)} %copy-done.16), kind=kOutput, calls=%fused_computation.48 | convolution fusion | flops 806617088 | bytes 2375744 | tf_op jit(solution)/shard_map/jh,jhp,jhn->hpn/dot_general | solution.py:42
  95.0 18.6 %all-to-all-done.1 = bf16[2,64,128,128]{3,1,0,2:T(8,128)(2,1)} async-done(((bf16[2,64,128,128]{3,1,0,2:T(8,128)(2,1)}), bf16[2,64,128,128]{3,1,0,2:T(8,128)(2,1)}, u32[]{:S(2)}, u32[]{:S(2)}) %all-to-all-start.1) | async-done | bytes 4194336 | tf_op jit(solution)/shard_map/all_to_all | solution.py:119
  113.6 3.3 %fusion.93 = (bf16[1,128,64,1,128]{4,2,0,1,3:T(8,128)(2,1)S(1)}, bf16[1,128,64,1,128]{4,2,0,1,3:T(8,128)(2,1)S(1)}) fusion(bf16[2,128,64,1,128]{4,2,0,1,3:T(8,128)(2,1)} %bitcast.21), kind=kLoop, calls=%fused_computation.95 | loop fusion | bytes 8388608 | tf_op jit(solution)/shard_map/slice | solution.py:138
  117.0 5.2 %maximum_bitcast_fusion = (bf16[8448,1,128]{2,0,1:T(8,128)(2,1)}, bf16[8448,1,128]{2,0,1:T(8,128)(2,1)S(1)}) fusion(bf16[256,128]{1,0:T(8,128)(2,1)S(1)} %copy-done.8, bf16[8192,128]{1,0:T(8,128)(2,1)S(1)} %bitcast.151, bf16[256,128]{1,0:T(8,128)(2,1)S(1)} %copy-done.7, bf16[8192,128]{1,0:T(8,128)(2,1)S(1)} %bitcast.150), kind=kLoop, calls=%fused_computation.30 | loop fusion | flops 8650752 | bytes 8650752 | tf_op jit(solution)/shard_map/reshape | solution.py:59
  122.2 63.6 %while.12 = (s32[]{:T(128)}, bf16[8,256,128]{2,1,0:T(8,128)(2,1)}, bf16[8,256,128]{1,2,0:T(8,128)(2,1)}, bf16[8448,1,128]{2,0,1:T(8,128)(2,1)}, bf16[8448,1,128]...) while((s32[]{:T(128)}, bf16[8,256,128]{2,1,0:T(8,128)(2,1)}, ...), condition=%wide.region_7.8_spmd.clone, body=%wide.region_4.7_spmd.clone.sunk | while | flops 1126825472 | bytes 30465628 | solution.py:84
  122.4 4.3 %fusion.105 = (f32[256]{0:T(256)S(1)}, f32[256,8448]{1,0:T(8,128)S(1)}) fusion(bf16[8448,1,128]{2,0,1:T(8,128)(2,1)} %get-tuple-element.212, bf16[8,256,128]{1,2,0:T(8,128)(2,1)} %get-tuple-element.211, s32[]{:T(128)} %get-tuple-element.200, s32[8448]{0:T(1024)S(1)} %get-tuple-element.214, pred[8448]{0:T(1024)(128)(4,1)S(1)} %get-tuple-element.215, ...), kind=kOutput, calls=%fused_computation.94.clone.1 | convolution fusion | flops 564461312 | bytes 10931200 | tf_op jit(solution)/shard_map/while/body/eval_jaxpr/dot_general | solution.py:72
  128.1 2.2 %fusion.107 = bf16[8,256,128]{2,1,0:T(8,128)(2,1)} fusion(bf16[8,256,128]{2,1,0:T(8,128)(2,1)} %get-tuple-element.201, s32[]{:T(128)} %get-tuple-element.200, bf16[8448,1,128]{2,0,1:T(8,128)(2,1)S(1)} %get-tuple-element.213, f32[256,8448]{1,0:T(8,128)S(1)} %get-tuple-element.189, f32[256]{0:T(256)S(1)} %get-tuple-element.190, f32[256]{0:T(256)S(1)} %fusion.106), kind=kOutput, calls=%fused_computation.17.clone.1 | convolution fusion | flops 558039040 | bytes 10881536 | tf_op jit(solution)/shard_map/while/body/eval_jaxpr/dot_general | solution.py:81
  130.4 4.3 %fusion.105 = (f32[256]{0:T(256)S(1)}, f32[256,8448]{1,0:T(8,128)S(1)}) fusion(bf16[8448,1,128]{2,0,1:T(8,128)(2,1)} %get-tuple-element.212, bf16[8,256,128]{1,2,0:T(8,128)(2,1)} %get-tuple-element.211, s32[]{:T(128)} %get-tuple-element.200, s32[8448]{0:T(1024)S(1)} %get-tuple-element.214, pred[8448]{0:T(1024)(128)(4,1)S(1)} %get-tuple-element.215, ...), kind=kOutput, calls=%fused_computation.94.clone.1 | convolution fusion | flops 564461312 | bytes 10931200 | tf_op jit(solution)/shard_map/while/body/eval_jaxpr/dot_general | solution.py:72
  138.3 4.3 %fusion.105 = (f32[256]{0:T(256)S(1)}, f32[256,8448]{1,0:T(8,128)S(1)}) fusion(bf16[8448,1,128]{2,0,1:T(8,128)(2,1)} %get-tuple-element.212, bf16[8,256,128]{1,2,0:T(8,128)(2,1)} %get-tuple-element.211, s32[]{:T(128)} %get-tuple-element.200, s32[8448]{0:T(1024)S(1)} %get-tuple-element.214, pred[8448]{0:T(1024)(128)(4,1)S(1)} %get-tuple-element.215, ...), kind=kOutput, calls=%fused_computation.94.clone.1 | convolution fusion | flops 564461312 | bytes 10931200 | tf_op jit(solution)/shard_map/while/body/eval_jaxpr/dot_general | solution.py:72
  146.2 4.3 %fusion.105 = (f32[256]{0:T(256)S(1)}, f32[256,8448]{1,0:T(8,128)S(1)}) fusion(bf16[8448,1,128]{2,0,1:T(8,128)(2,1)} %get-tuple-element.212, bf16[8,256,128]{1,2,0:T(8,128)(2,1)} %get-tuple-element.211, s32[]{:T(128)} %get-tuple-element.200, s32[8448]{0:T(1024)S(1)} %get-tuple-element.214, pred[8448]{0:T(1024)(128)(4,1)S(1)} %get-tuple-element.215, ...), kind=kOutput, calls=%fused_computation.94.clone.1 | convolution fusion | flops 564461312 | bytes 10931200 | tf_op jit(solution)/shard_map/while/body/eval_jaxpr/dot_general | solution.py:72
  151.9 2.2 %fusion.107 = bf16[8,256,128]{2,1,0:T(8,128)(2,1)} fusion(bf16[8,256,128]{2,1,0:T(8,128)(2,1)} %get-tuple-element.201, s32[]{:T(128)} %get-tuple-element.200, bf16[8448,1,128]{2,0,1:T(8,128)(2,1)S(1)} %get-tuple-element.213, f32[256,8448]{1,0:T(8,128)S(1)} %get-tuple-element.189, f32[256]{0:T(256)S(1)} %get-tuple-element.190, f32[256]{0:T(256)S(1)} %fusion.106), kind=kOutput, calls=%fused_computation.17.clone.1 | convolution fusion | flops 558039040 | bytes 10881536 | tf_op jit(solution)/shard_map/while/body/eval_jaxpr/dot_general | solution.py:81
  154.1 4.3 %fusion.105 = (f32[256]{0:T(256)S(1)}, f32[256,8448]{1,0:T(8,128)S(1)}) fusion(bf16[8448,1,128]{2,0,1:T(8,128)(2,1)} %get-tuple-element.212, bf16[8,256,128]{1,2,0:T(8,128)(2,1)} %get-tuple-element.211, s32[]{:T(128)} %get-tuple-element.200, s32[8448]{0:T(1024)S(1)} %get-tuple-element.214, pred[8448]{0:T(1024)(128)(4,1)S(1)} %get-tuple-element.215, ...), kind=kOutput, calls=%fused_computation.94.clone.1 | convolution fusion | flops 564461312 | bytes 10931200 | tf_op jit(solution)/shard_map/while/body/eval_jaxpr/dot_general | solution.py:72
  162.0 4.3 %fusion.105 = (f32[256]{0:T(256)S(1)}, f32[256,8448]{1,0:T(8,128)S(1)}) fusion(bf16[8448,1,128]{2,0,1:T(8,128)(2,1)} %get-tuple-element.212, bf16[8,256,128]{1,2,0:T(8,128)(2,1)} %get-tuple-element.211, s32[]{:T(128)} %get-tuple-element.200, s32[8448]{0:T(1024)S(1)} %get-tuple-element.214, pred[8448]{0:T(1024)(128)(4,1)S(1)} %get-tuple-element.215, ...), kind=kOutput, calls=%fused_computation.94.clone.1 | convolution fusion | flops 564461312 | bytes 10931200 | tf_op jit(solution)/shard_map/while/body/eval_jaxpr/dot_general | solution.py:72
  170.0 4.3 %fusion.105 = (f32[256]{0:T(256)S(1)}, f32[256,8448]{1,0:T(8,128)S(1)}) fusion(bf16[8448,1,128]{2,0,1:T(8,128)(2,1)} %get-tuple-element.212, bf16[8,256,128]{1,2,0:T(8,128)(2,1)} %get-tuple-element.211, s32[]{:T(128)} %get-tuple-element.200, s32[8448]{0:T(1024)S(1)} %get-tuple-element.214, pred[8448]{0:T(1024)(128)(4,1)S(1)} %get-tuple-element.215, ...), kind=kOutput, calls=%fused_computation.94.clone.1 | convolution fusion | flops 564461312 | bytes 10931200 | tf_op jit(solution)/shard_map/while/body/eval_jaxpr/dot_general | solution.py:72
  177.9 4.3 %fusion.105 = (f32[256]{0:T(256)S(1)}, f32[256,8448]{1,0:T(8,128)S(1)}) fusion(bf16[8448,1,128]{2,0,1:T(8,128)(2,1)} %get-tuple-element.212, bf16[8,256,128]{1,2,0:T(8,128)(2,1)} %get-tuple-element.211, s32[]{:T(128)} %get-tuple-element.200, s32[8448]{0:T(1024)S(1)} %get-tuple-element.214, pred[8448]{0:T(1024)(128)(4,1)S(1)} %get-tuple-element.215, ...), kind=kOutput, calls=%fused_computation.94.clone.1 | convolution fusion | flops 564461312 | bytes 10931200 | tf_op jit(solution)/shard_map/while/body/eval_jaxpr/dot_general | solution.py:72
  (87 shorter events, 45.7 us)
Async XLA Ops:
  7.2 1.2 copy-start
  10.3 39.1 %all-to-all-start = ((bf16[16,16,4,256]{3,2,1,0:T(4,128)(2,1)}), bf16[16,16,4,256]{3,2,1,0:T(4,128)(2,1)S(1)}, u32[]{:S(2)}, u32[]{:S(2)}) async-start(bf16[16,16,4,256]{3,2,1,0:T(4,128)(2,1)} %gather_fusion), calls=%async_computation | async-start | bytes 1048576 | tf_op jit(solution)/shard_map/all_to_all | solution.py:109
  34.8 5.5 %copy-start.9 = (f32[1,256,16]{1,2,0:T(8,128)S(1)}, f32[1,256,16]{1,2,0:T(8,128)}, u32[]{:S(2)}) copy-start(f32[1,256,16]{1,2,0:T(8,128)} %param.22) | copy-start | bytes 49156
  34.8 5.5 %copy-start.14 = (f32[16]{0:T(128)S(1)}, f32[16]{0:T(128)}, u32[]{:S(2)}) copy-start(f32[16]{0:T(128)} %param.23) | copy-start | bytes 196
  34.8 5.5 %copy-start.15 = (f32[16]{0:T(128)S(1)}, f32[16]{0:T(128)}, u32[]{:S(2)}) copy-start(f32[16]{0:T(128)} %param.24) | copy-start | bytes 196
  49.4 12.0 %copy-start.3 = (bf16[1,256,1024]{2,1,0:T(8,128)(2,1)S(1)}, bf16[1,256,1024]{2,1,0:T(8,128)(2,1)}, u32[]{:S(2)}) copy-start(bf16[1,256,1024]{2,1,0:T(8,128)(2,1)} %param.29) | copy-start | bytes 1572868
  49.4 13.1 %copy-start.4 = (bf16[1,256,1024]{2,1,0:T(8,128)(2,1)S(1)}, bf16[1,256,1024]{2,1,0:T(8,128)(2,1)}, u32[]{:S(2)}) copy-start(bf16[1,256,1024]{2,1,0:T(8,128)(2,1)} %param.18) | copy-start | bytes 1572868
  49.4 13.3 %copy-start.2 = (bf16[1,256,1024]{2,1,0:T(8,128)(2,1)S(1)}, bf16[1,256,1024]{2,1,0:T(8,128)(2,1)}, u32[]{:S(2)}) copy-start(bf16[1,256,1024]{2,1,0:T(8,128)(2,1)} %param.19) | copy-start | bytes 1572868
  49.4 16.2 %copy-start.6 = (bf16[1,256,256]{2,1,0:T(8,128)(2,1)S(1)}, bf16[1,256,256]{2,1,0:T(8,128)(2,1)}, u32[]{:S(2)}) copy-start(bf16[1,256,256]{2,1,0:T(8,128)(2,1)} %param.21) | copy-start | bytes 393220
  49.4 64.2 %all-to-all-start.1 = ((bf16[2,64,128,128]{3,1,0,2:T(8,128)(2,1)}), bf16[2,64,128,128]{3,1,0,2:T(8,128)(2,1)}, u32[]{:S(2)}, u32[]{:S(2)}) async-start(bf16[2,64,128,128]{3,1,0,2:T(8,128)(2,1)} %copy.62), calls=%async_computation.2 | async-start | bytes 8388608 | tf_op jit(solution)/shard_map/all_to_all | solution.py:119
  61.0 5.3 %copy-start.5 = (bf16[1,256,256]{2,1,0:T(8,128)(2,1)S(1)}, bf16[1,256,256]{2,1,0:T(8,128)(2,1)}, u32[]{:S(2)}) copy-start(bf16[1,256,256]{2,1,0:T(8,128)(2,1)} %param.20) | copy-start | bytes 393220
  61.0 127.3 %reduce-scatter.2.cloned.1.call-start = ((), (), s32[]{:S(2)}) async-start(), calls=%async_computation.3 | async-start | bytes 4718592 | tf_op jit(solution)/shard_map/reduce_scatter | solution.py:134
  67.5 5.5 %copy-start.11 = (f32[256,16]{0,1:T(8,128)S(1)}, f32[256,16]{0,1:T(8,128)}, u32[]{:S(2)}) copy-start(f32[256,16]{0,1:T(8,128)} %get-tuple-element.129) | copy-start | bytes 49156
  67.5 5.5 %copy-start.18 = (f32[16]{0:T(128)S(1)}, f32[16]{0:T(128)}, u32[]{:S(2)}) copy-start(f32[16]{0:T(128)} %param.25) | copy-start | bytes 196
  73.0 5.9 %copy-start.17 = (f32[1024]{0:T(1024)S(1)}, f32[1024]{0:T(1024)}, u32[]{:S(2)}) copy-start(f32[1024]{0:T(1024)} %param.26) | copy-start | bytes 12292
  91.1 0.6 copy-start.16
  113.6 3.3 %copy-start.7 = (bf16[256,128]{1,0:T(8,128)(2,1)S(1)}, bf16[256,128]{1,0:T(8,128)(2,1)}, u32[]{:S(2)}) copy-start(bf16[256,128]{1,0:T(8,128)(2,1)} %get-tuple-element.125) | copy-start | bytes 196612
  113.6 3.4 %copy-start.8 = (bf16[256,128]{1,0:T(8,128)(2,1)S(1)}, bf16[256,128]{1,0:T(8,128)(2,1)}, u32[]{:S(2)}) copy-start(bf16[256,128]{1,0:T(8,128)(2,1)} %get-tuple-element.126) | copy-start | bytes 196612
  117.0 5.2 %copy-start.10 = (s32[8448]{0:T(1024)S(1)}, s32[8448]{0:T(1024)}, u32[]{:S(2)}) copy-start(s32[8448]{0:T(1024)} %iota_add_fusion) | copy-start | bytes 101380
  117.0 5.2 %copy-start.12 = (pred[8448]{0:T(1024)(128)(4,1)S(1)}, pred[8448]{0:T(1024)(128)(4,1)}, u32[]{:S(2)}) copy-start(pred[8448]{0:T(1024)(128)(4,1)} %get-tuple-element.197) | copy-start | bytes 25348
  117.0 5.2 %copy-start.13 = (pred[8448]{0:T(1024)(128)(4,1)S(1)}, pred[8448]{0:T(1024)(128)(4,1)}, u32[]{:S(2)}) copy-start(pred[8448]{0:T(1024)(128)(4,1)} %get-tuple-element.198) | copy-start | bytes 25348
  185.8 2.5 %copy-start.1 = (f32[16,16,4,256]{3,2,1,0:T(4,128)S(1)}, f32[16,16,4,256]{3,2,1,0:T(4,128)}, u32[]{:S(2)}) copy-start(f32[16,16,4,256]{3,2,1,0:T(4,128)} %param.28) | copy-start | bytes 3145732
Sparse Core Ops, SparseCore 0:
  91.3 45.0 reduce-scatter.1
where the time goes:
time: 196 us; the launch traced here: 195 us
  matrix products  78.1 us (40%)
  local copies, waits for them, and re-layouts  40 us (20%)
  other arithmetic  22.5 us (11%)
  starting transfers between devices  19.4 us (10%)
  waiting for transfers between devices  18.6 us (9%)
  between operations  16.2 us (8%)
    dot_general x8, matrix products, one_head(): lax.dot_general(q_one, k_one, (((1,), (1,)), ((), ())), preferred_element...  34.3 us
    all_to_all x1, waiting for transfers between devices, local(): lax.all_to_all(arranged, ('traj', 'tensor'), split_axis=2, concat_axis=1,...  18.6 us
    dot_general x8, matrix products, one_head(): jnp.dot(expo.astype(jnp.bfloat16), v_one, preferred_element_type=jnp.floa...  17.8 us
    reshape x2, local copies, waits for them, and re-layouts, local(): jnp.transpose(arranged, (0, 2, 1, 3, 4))  12.4 us
    dot_general x1, matrix products, local(): jnp.dot(normed, out_weight, preferred_element_type=jnp.float32)[None]  12.2 us
    all_to_all x1, starting transfers between devices, local(): lax.all_to_all(arranged, ('traj', 'tensor'), split_axis=2, concat_axis=1,...  11.6 us
    reduce_sum x8, other arithmetic, one_head(): total = jnp.sum(expo, axis=1, keepdims=True)  11.2 us
    unnamed x41, local copies, waits for them, and re-layouts  7.63 us
  transfers between devices with their start and end apart: 3, of which 1 were waited for; matrix products, arithmetic and copies ran while one was open for 70% of the time, Pallas kernels for 0%

commit v1 on v0

v1 whole, which is shorter than its diff:
```python
import functools
import math

import jax
import jax.numpy as jnp
from jax import lax
from jax.experimental import pallas as pl
from jax.experimental.pallas import tpu as pltpu
from jax.sharding import PartitionSpec as P

HEAD_DIM = 64
STATE = 256
ATT_DIM = 128
ROWS = 64
CHUNKS = ((0, 32), (32, 32))
KEY_BLOCK = 1024
VMEM_LIMIT = 48 * 1024 * 1024
NEG = -1e30


def pack_kernel(order_ref, kv_ref, *refs):
    outs, sem = refs[:-1], refs[-1]
    slots = kv_ref.shape[1]
    tensor = kv_ref.shape[3] // ATT_DIM

    def copies(slot):
        taken = order_ref[slot]
        for number, ((first, rows), out) in enumerate(zip(CHUNKS, outs)):
            for h in range(tensor):
                yield pltpu.make_async_copy(
                    kv_ref.at[:, taken, pl.ds(first, rows), pl.ds(h * ATT_DIM, ATT_DIM)],
                    out.at[slot * tensor + h],
                    sem.at[number],
                )

    for slot in range(slots):
        for copy in copies(slot):
            copy.start()
    for number, out in enumerate(outs):
        pltpu.make_async_copy(out, out, sem.at[number]).wait()


def pack(order, prefix_kv):
    slots = prefix_kv.shape[1]
    tensor = prefix_kv.shape[3] // ATT_DIM
    return pl.pallas_call(
        pack_kernel,
        out_shape=[
            jax.ShapeDtypeStruct((slots * tensor, 2, rows, ATT_DIM), jnp.bfloat16)
            for _, rows in CHUNKS
        ],
        in_specs=[pl.BlockSpec(memory_space=pltpu.SMEM), pl.BlockSpec(memory_space=pl.ANY)],
        out_specs=[pl.BlockSpec(memory_space=pl.ANY) for _ in CHUNKS],
        scratch_shapes=[pltpu.SemaphoreType.DMA((len(CHUNKS),))],
        compiler_params=pltpu.CompilerParams(vmem_limit_bytes=VMEM_LIMIT),
        cost_estimate=pl.CostEstimate(flops=0, bytes_accessed=8 << 20, transcendentals=0),
        name="pack_prefix",
    )(order, prefix_kv)


def mixer_kernel(
    x_ref, gate_ref, b_ref, c_ref, dt_ref, bias_ref, rate_ref, skip_ref, gain_ref, state_ref, w_ref,
    out_ref, final_ref, normed, y_ref, xt_ref,
):
    seg, width = x_ref.shape
    heads = dt_ref.shape[1]
    f32, bf16 = jnp.float32, jnp.bfloat16

    @pl.when(pl.program_id(0) == 0)
    def _():
        raw = dt_ref[...] + bias_ref[...]
        step = jnp.maximum(raw, 0.0) + jnp.log1p(jnp.exp(-jnp.abs(raw)))
        rows = lax.broadcasted_iota(jnp.int32, (seg, seg), 0)
        cols = lax.broadcasted_iota(jnp.int32, (seg, seg), 1)
        causal = rows >= cols
        lower = jnp.where(causal, 1.0, 0.0).astype(f32)
        pad = jnp.zeros((seg, 128 - heads), f32)
        decay = jnp.concatenate([-step * rate_ref[...], pad], axis=1)
        cum = jnp.dot(lower, decay, precision=lax.Precision.HIGHEST, preferred_element_type=f32)
        step = jnp.concatenate([step, pad], axis=1)
        cum_t = cum.T
        step_t = step.T
        last = cum[seg - 1 : seg, :]
        grow = jnp.exp(cum)
        tail = jnp.exp(last - cum) * step
        keep = jnp.exp(last)
        c = c_ref[...]
        b = b_ref[...]
        inner = lax.dot_general(c, b, (((1,), (1,)), ((), ())), preferred_element_type=f32)
        inner = jnp.where(causal, inner, 0.0)
        lane = lax.broadcasted_iota(jnp.int32, (seg, 128), 1)
        square = jnp.zeros((seg, 1), f32)
        for p in range(heads // 2):
            h = 2 * p
            span = pl.ds(p * 128, 128)
            x = x_ref[:, span]
            x_f = x.astype(f32)
            first = lane < HEAD_DIM

            def mixed_with(k):
                diff = jnp.minimum(cum[:, k : k + 1] - cum_t[k : k + 1, :], 0.0)
                mix = jnp.exp(diff) * inner * step_t[k : k + 1, :]
                return jnp.dot(mix.astype(bf16), x, preferred_element_type=f32)

            def spread(a):
                return jnp.where(first, a[:, h : h + 1], a[:, h + 1 : h + 2])

            carried = lax.dot_general(
                c, state_ref[span, :], (((1,), (1,)), ((), ())), preferred_element_type=f32
            )
            y = jnp.where(first, mixed_with(h), mixed_with(h + 1))
            y = y + spread(grow) * carried + skip_ref[:, span] * x_f
            gate = gate_ref[:, span].astype(f32)
            gated = y * (gate / (1.0 + jnp.exp(-gate)))
            y_ref[:, span] = gated
            square = square + jnp.sum(gated * gated, axis=1, keepdims=True)
            xt_ref[:, span] = (x_f * spread(tail)).astype(bf16)
        factor = lax.rsqrt(square / width + 1e-05)
        normed[...] = (y_ref[...] * factor * gain_ref[...]).astype(bf16)
        added = lax.dot_general(xt_ref[...], b, (((0,), (0,)), ((), ())), preferred_element_type=f32)
        for h in range(heads):
            span = pl.ds(h * HEAD_DIM, HEAD_DIM)
            final_ref[span, :] = (
                keep[:, h : h + 1] * state_ref[span, :].astype(f32)
                + added[h * HEAD_DIM : (h + 1) * HEAD_DIM]
            )

    out_ref[...] = jnp.dot(normed[...], w_ref[...], preferred_element_type=f32).astype(bf16)


def mixer(x, gate, b, c, dt, bias, rate, skip, gain, state, weight):
    seg, width = x.shape
    heads = dt.shape[1]
    total = weight.shape[1]
    block = 1024

    def whole(a):
        return pl.BlockSpec(a.shape, lambda i: (0,) * a.ndim)

    small = (
        x, gate, b, c, dt, bias[None], rate[None], jnp.repeat(skip, HEAD_DIM)[None], gain[None], state
    )
    return pl.pallas_call(
        mixer_kernel,
        grid=(total // block,),
        in_specs=[whole(a) for a in small] + [pl.BlockSpec((width, block), lambda i: (0, i))],
        out_specs=[
            pl.BlockSpec((seg, block), lambda i: (0, i)),
            pl.BlockSpec((width, STATE), lambda i: (0, 0)),
        ],
        out_shape=[
            jax.ShapeDtypeStruct((seg, total), jnp.bfloat16),
            jax.ShapeDtypeStruct((width, STATE), jnp.float32),
        ],
        scratch_shapes=[
            pltpu.VMEM((seg, width), jnp.bfloat16),
            pltpu.VMEM((seg, width), jnp.float32),
            pltpu.VMEM((seg, width), jnp.bfloat16),
        ],
        compiler_params=pltpu.CompilerParams(vmem_limit_bytes=VMEM_LIMIT),
        cost_estimate=pl.CostEstimate(
            flops=2 * seg * width * total + 4 * seg * seg * width,
            bytes_accessed=2 * width * total + 6 * seg * total,
            transcendentals=heads * seg * seg,
        ),
        name="mamba_mixer",
    )(*small, weight)


def attend_kernel(
    first_row, rows, first, last, length_ref, q_ref, kv_ref, *refs
):
    f32, bf16 = jnp.float32, jnp.bfloat16
    if first:
        new_ref, refs = refs[0], refs[1:]
        outs, refs = refs[: 1 if last else 3], refs[1 if last else 3 :]
    else:
        carry, outs, refs = refs[:3], refs[3 : 4 if last else 6], refs[4 if last else 6 :]
    top_ref, sum_ref, acc_ref, qt_ref = refs
    heads = q_ref.shape[1] // ATT_DIM
    seg = q_ref.shape[0]
    step = pl.program_id(0)
    sources = kv_ref.shape[0]
    block = sources * rows

    def scores(h, keys2):
        return jnp.dot(keys2, qt_ref[h], preferred_element_type=f32)

    def update(keys, values, mask, start):
        keys2 = jnp.concatenate([keys, keys], axis=1)
        size = values.shape[0]
        ones = jnp.ones((size, 16), bf16)
        values_t = jnp.concatenate([values.T, ones.T], axis=0)
        for h in range(heads):
            s = scores(h, keys2)
            if mask is not None:
                s = jnp.where(mask, s, NEG)
            peak = jnp.max(s, axis=0, keepdims=True)
            if start:
                top = peak
            else:
                old = top_ref[h : h + 1, :]
                top = jnp.maximum(old, peak)
                scale = jnp.exp2(old - top)
            top_ref[h : h + 1, :] = top
            weights = jnp.exp2(s - top).astype(bf16)
            part = jnp.dot(values_t, weights, preferred_element_type=f32)
            if start:
                acc_ref[h] = part[:ATT_DIM]
                sum_ref[h : h + 1, :] = part[ATT_DIM : ATT_DIM + 1]
            else:
                acc_ref[h] = acc_ref[h] * scale + part[:ATT_DIM]
                sum_ref[h : h + 1, :] = (
                    sum_ref[h : h + 1, :] * scale + part[ATT_DIM : ATT_DIM + 1]
                )

    @pl.when(step == 0)
    def _():
        factor = math.log2(math.e) / math.sqrt(ATT_DIM)
        for h in range(heads):
            q = q_ref[:, h * ATT_DIM : (h + 1) * ATT_DIM].astype(f32).T * factor
            high = q.astype(bf16)
            qt_ref[h, :ATT_DIM, :] = high
            qt_ref[h, ATT_DIM:, :] = (q - high.astype(f32)).astype(bf16)
        if first:
            keys = lax.broadcasted_iota(jnp.int32, (seg, seg), 0)
            tokens = lax.broadcasted_iota(jnp.int32, (seg, seg), 1)
            update(new_ref[0], new_ref[1], keys <= tokens, True)
        else:
            top_ref[...] = carry[0][...]
            sum_ref[...] = carry[1][...]
            acc_ref[...] = carry[2][...]

    length = length_ref[0]
    start = step * sources * ROWS + first_row
    end = start + (sources - 1) * ROWS + rows

    def block_of(which):
        return kv_ref[:, which].reshape(block, ATT_DIM)

    @pl.when(end <= length)
    def _():
        update(block_of(0), block_of(1), None, False)

    @pl.when((start < length) & (end > length))
    def _():
        row = lax.broadcasted_iota(jnp.int32, (block, seg), 0)
        place = start + row // rows * ROWS + row % rows
        update(block_of(0), block_of(1), place < length, False)

    @pl.when(step == pl.num_programs(0) - 1)
    def _():
        if last:
            for h in range(heads):
                result = acc_ref[h] / sum_ref[h : h + 1, :]
                outs[0][:, h * ATT_DIM : (h + 1) * ATT_DIM] = result.T.astype(bf16)
        else:
            outs[0][...] = top_ref[...]
            outs[1][...] = sum_ref[...]
            outs[2][...] = acc_ref[...]


def attend(length, queries, kv, new_kv, carry, first_row, last):
    seg, width = queries.shape
    heads = width // ATT_DIM
    sources, _, rows, _ = kv.shape
    per = KEY_BLOCK // rows
    first = carry is None

    def whole(shape):
        return pl.BlockSpec(shape, lambda i, n: (0,) * len(shape))

    carried = ((heads, seg), (heads, seg), (heads, ATT_DIM, seg))
    more = (new_kv,) if first else carry
    outs = ((seg, width),) if last else carried
    kinds = (jnp.bfloat16,) if last else (jnp.float32,) * 3

    def at(i, n):
        return (jnp.minimum(i, (n[0] - 1 - first_row) // (per * ROWS)), 0, 0, 0)

    work = sources * rows * seg * heads
    result = pl.pallas_call(
        functools.partial(attend_kernel, first_row, rows, first, last),
        grid_spec=pltpu.PrefetchScalarGridSpec(
            num_scalar_prefetch=1,
            grid=(sources // per,),
            in_specs=[whole(queries.shape), pl.BlockSpec((per, 2, rows, ATT_DIM), at)]
            + [whole(a.shape) for a in more],
            out_specs=[whole(s) for s in outs],
            scratch_shapes=[
                pltpu.VMEM((heads, seg), jnp.float32),
                pltpu.VMEM((heads, seg), jnp.float32),
                pltpu.VMEM((heads, ATT_DIM, seg), jnp.float32),
                pltpu.VMEM((heads, 2 * ATT_DIM, seg), jnp.bfloat16),
            ],
        ),
        out_shape=[jax.ShapeDtypeStruct(s, k) for s, k in zip(outs, kinds)],
        compiler_params=pltpu.CompilerParams(vmem_limit_bytes=VMEM_LIMIT),
        cost_estimate=pl.CostEstimate(
            flops=8 * work * ATT_DIM, bytes_accessed=4 * sources * rows * ATT_DIM, transcendentals=work
        ),
        name="attend_chunk",
    )(length[None], queries, kv, *more)
    return result[0] if last else tuple(result)


def local(
    ssm_in,
    gate_in,
    b_in,
    c_in,
    dt_in,
    dt_bias,
    decay_rate,
    skip,
    norm_gain,
    out_weight,
    state_roll,
    query,
    new_kv,
    prefix_kv,
    prefix_len,
    order,
):
    slot = lax.axis_index("traj")
    taken = lax.dynamic_index_in_dim(order, slot, 0, keepdims=False)
    length = lax.dynamic_index_in_dim(prefix_len, taken, 0, keepdims=False)
    own_state = lax.all_to_all(
        state_roll[order].astype(jnp.bfloat16), "traj", split_axis=0, concat_axis=0, tiled=True
    )
    packed = pack(order, prefix_kv)
    received = [
        lax.all_to_all(part, ("traj", "tensor"), split_axis=0, concat_axis=0, tiled=True)
        for part in packed
    ]
    heads = dt_in.shape[2]
    state = jnp.transpose(own_state, (1, 0, 2, 3)).reshape(heads * HEAD_DIM, STATE)
    product, final = mixer(
        ssm_in[0],
        gate_in[0],
        b_in[0],
        c_in[0],
        dt_in[0],
        dt_bias,
        decay_rate,
        skip,
        norm_gain,
        state,
        out_weight,
    )
    mixed = lax.psum_scatter(product[None], "tensor", scatter_dimension=2, tiled=True)
    carry = None
    for number, (part, (first_row, _)) in enumerate(zip(received, CHUNKS)):
        last = number == len(CHUNKS) - 1
        carry = attend(length, query[0], part, new_kv[:, 0], carry, first_row, last)
    return (mixed, final.reshape(1, heads, HEAD_DIM, STATE), carry[None])


def solution(mesh):
    in_specs = (
        P("traj", None, "tensor"),
        P("traj", None, "tensor"),
        P("traj", None, "tensor"),
        P("traj", None, "tensor"),
        P("traj", None, "tensor"),
        P("tensor"),
        P("tensor"),
        P("tensor"),
        P("tensor"),
        P("tensor", None),
        P(None, "tensor", "traj", None),
        P("traj", None, "tensor"),
        P(None, "traj", None, "tensor"),
        P(None, None, ("traj", "tensor"), None),
        P(),
        P(),
    )
    out_specs = (
        P("traj", None, "tensor"),
        P("traj", "tensor", None, None),
        P("traj", None, "tensor"),
    )
    return jax.shard_map(local, mesh=mesh, in_specs=in_specs, out_specs=out_specs, check_vma=False)
```

time: 196 us -> 163 us (0.83)
  the two profiles are of different devices: /device:TPU:1 before, /device:TPU:27 now
where the time goes in v1:
time: 163 us; the launch traced here: 161 us
  Pallas kernels  71.1 us (44%)
  blocking collectives  38.6 us (24%)
  between operations  16.2 us (10%)
  starting transfers between devices  14.1 us (9%)
  local copies, waits for them, and re-layouts  12.7 us (8%)
  waiting for transfers between devices  7.47 us (5%)
    pallas_call x2, Pallas kernels, attend(): pl.pallas_call(functools.partial(attend_kernel, first_row, rows, first, l...  51.4 us
    all_to_all x1, blocking collectives, local(): lax.all_to_all(part, ('traj', 'tensor'), split_axis=0, concat_axis=0, til...  38.6 us
    pallas_call x1, Pallas kernels, mixer(): pl.pallas_call(mixer_kernel, grid=(total // block,), in_specs=[whole(a) f...  16.8 us
    unnamed x41, local copies, waits for them, and re-layouts  9.06 us
    all_to_all x1, starting transfers between devices, local(): lax.all_to_all(part, ('traj', 'tensor'), split_axis=0, concat_axis=0, til...  7.46 us
    all_to_all x1, waiting for transfers between devices, local(): lax.all_to_all(state_roll[order].astype(jnp.bfloat16), 'traj', split_axis...  7.45 us
    all_to_all x1, starting transfers between devices, local(): lax.all_to_all(state_roll[order].astype(jnp.bfloat16), 'traj', split_axis...  6.58 us
  transfers between devices with their start and end apart: 3, of which 1 were waited for; matrix products, arithmetic and copies ran while one was open for 1% of the time, Pallas kernels for 34%

profile of v1, /device:TPU:27, one launch (start us, length us, event | category | flops | bytes accessed | tf_op | source)
XLA Modules:
  0.0 160.9 jit_solution(7746399841198638430)
XLA Ops:
  7.2 0.7 compare_select_fusion
  8.0 0.5 copy-done
  8.5 1.9 %gather_fusion = bf16[16,16,4,256]{3,2,1,0:T(4,128)(2,1)} fusion(f32[16,16,4,256]{3,2,1,0:T(4,128)S(1)} %copy-done, s32[1024]{0:T(1024)S(1)} %pad_clamp_fusion), kind=kCustom, calls=%fused_computation | custom fusion | bytes 1048640 | tf_op jit(solution)/shard_map/gather | solution.py:329
  10.4 6.6 %all-to-all-start = ((bf16[16,16,4,256]{3,2,1,0:T(4,128)(2,1)}), bf16[16,16,4,256]{3,2,1,0:T(4,128)(2,1)S(1)}, u32[]{:S(2)}, u32[]{:S(2)}) async-start(bf16[16,16,4,256]{3,2,1,0:T(4,128)(2,1)} %gather_fusion), calls=%async_computation | async-start | bytes 1048576 | tf_op jit(solution)/shard_map/all_to_all | solution.py:328
  17.0 0.1 copy.19
  17.2 0.1 broadcast_in_dim_reshape.3.skip_ref
  17.3 7.5 %all-to-all-done = bf16[16,16,4,256]{3,2,1,0:T(4,128)(2,1)S(1)} async-done(((bf16[16,16,4,256]{3,2,1,0:T(4,128)(2,1)}), bf16[16,16,4,256]{3,2,1,0:T(4,128)(2,1)S(1)}, u32[]{:S(2)}, u32[]{:S(2)}) %all-to-all-start) | async-done | bytes 524320 | tf_op jit(solution)/shard_map/all_to_all | solution.py:328
  24.7 0.2 copy.20
  24.9 0.1 reshape.12.state_ref
  25.2 16.8 %mamba_mixer.1 = (bf16[256,8192]{1,0:T(8,128)(2,1)S(1)}, f32[1024,256]{1,0:T(8,128)}) custom-call(bf16[256,1024]{1,0:T(8,128)(2,1)S(1)} %bitcast.17, bf16[256,1024]{1,0:T(8,128)(2,1)S(1)} %bitcast.18, bf16[256,256]{1,0:T(8,128)(2,1)S(1)} %bitcast.19, bf16[256,256]{1,0:T(8,128)(2,1)S(1)} %bitcast.20, f32[256,16]{1,0:T(8,128)S(1)} %bitcast.16, ...), custom_call_target="tpu_custom_call" | custom-call | flops 4563402752 | bytes 29360128 | tf_op jit(solution)/shard_map/mamba_mixer/pallas_call | solution.py:143
  41.9 1.9 %copy-done.1 = bf16[256,8192]{1,0:T(8,128)(2,1)} copy-done((bf16[256,8192]{1,0:T(8,128)(2,1)}, bf16[256,8192]{1,0:T(8,128)(2,1)S(1)}, u32[]{:S(2)}) %copy-start.1) | copy-done | bytes 4194328
  43.9 0.6 copy-done.11
  44.6 2.9 %pack_prefix.1 = (bf16[128,2,32,128]{3,2,1,0:T(8,128)(2,1)S(1)}, bf16[128,2,32,128]{3,2,1,0:T(8,128)(2,1)S(1)}) custom-call(s32[16]{0:T(128)S(1)} %copy-done.11, bf16[2,16,64,1024]{3,2,1,0:T(8,128)(2,1)} %kv_ref.1), custom_call_target="tpu_custom_call" | custom-call | bytes 8388608 | tf_op jit(solution)/shard_map/pack_prefix/pallas_call | solution.py:46
  47.4 38.6 %all_to_all.15.kv_ref = bf16[128,2,32,128]{3,2,1,0:T(8,128)(2,1)} all-to-all(bf16[128,2,32,128]{3,2,1,0:T(8,128)(2,1)S(1)} %get-tuple-element.13), channel_id=1, replica_groups=mesh['traj'=16,'tensor'=8] {'traj','tensor'}, dimensions={0} | all-to-all | bytes 4194304 | tf_op jit(solution)/shard_map/all_to_all | solution.py:333
  86.1 7.5 %all-to-all-start.1 = ((bf16[128,2,32,128]{3,2,1,0:T(8,128)(2,1)}), bf16[128,2,32,128]{3,2,1,0:T(8,128)(2,1)S(1)}, u32[]{:S(2)}, u32[]{:S(2)}) async-start(bf16[128,2,32,128]{3,2,1,0:T(8,128)(2,1)} %copy-done.2), calls=%async_computation.2 | async-start | bytes 4194304 | tf_op jit(solution)/shard_map/all_to_all | solution.py:333
  93.5 0.6 dynamic_slice.7
  96.1 0.7 dynamic_slice.8.length_ref
  96.7 1.6 copy-done.3
  98.3 1.0 copy-done.12
  99.4 26.2 %attend_chunk.2 = (f32[8,256]{1,0:T(8,128)S(1)}, f32[8,256]{1,0:T(8,128)S(1)}, f32[8,128,256]{2,1,0:T(8,128)S(1)}) custom-call(s32[1]{0:T(128)} %dynamic_slice.8.length_ref, bf16[256,1024]{1,0:T(8,128)(2,1)S(1)} %bitcast.24, bf16[128,2,32,128]{3,2,1,0:T(8,128)(2,1)S(1)} %copy-done.3, bf16[2,256,128]{2,1,0:T(8,128)(2,1)S(1)} %bitcast.26), custom_call_target="tpu_custom_call" | custom-call | flops 8589934592 | bytes 2097152 | tf_op jit(solution)/shard_map/attend_chunk/pallas_call | solution.py:282
  125.6 1.0 copy-done.15
  126.5 1.0 copy-done.13
  127.6 1.2 copy-done.16
  128.8 25.2 %attend_chunk.3 = bf16[256,1024]{1,0:T(8,128)(2,1)} custom-call(s32[1]{0:T(128)} %dynamic_slice.8.length_ref, bf16[256,1024]{1,0:T(8,128)(2,1)S(1)} %bitcast.25, bf16[128,2,32,128]{3,2,1,0:T(8,128)(2,1)S(1)} %all-to-all-done.1.kv_ref, f32[8,256]{1,0:T(8,128)S(1)} %get-tuple-element.14.refs_0_, f32[8,256]{1,0:T(8,128)S(1)} %get-tuple-element.15.refs_1_, ...), custom_call_target="tpu_custom_call" | custom-call | flops 8589934592 | bytes 2097152 | tf_op jit(solution)/shard_map/attend_chunk/pallas_call | solution.py:282
  (38 shorter events, 0.2 us)
Async XLA Ops:
  7.2 1.2 copy-start
  7.2 9.8 %copy-start.17 = (f32[1,256,16]{1,2,0:T(8,128)S(1)}, f32[1,256,16]{1,2,0:T(8,128)}, u32[]{:S(2)}) copy-start(f32[1,256,16]{1,2,0:T(8,128)} %param.20) | copy-start | bytes 49156
  7.2 9.9 %copy-start.18 = (f32[16]{0:T(128)S(1)}, f32[16]{0:T(128)}, u32[]{:S(2)}) copy-start(f32[16]{0:T(128)} %param.23) | copy-start | bytes 196
  8.4 16.7 %copy-start.4 = (bf16[1,256,1024]{2,1,0:T(8,128)(2,1)S(1)}, bf16[1,256,1024]{2,1,0:T(8,128)(2,1)}, u32[]{:S(2)}) copy-start(bf16[1,256,1024]{2,1,0:T(8,128)(2,1)} %param.16) | copy-start | bytes 1572868
  8.4 16.7 %copy-start.5 = (bf16[1,256,1024]{2,1,0:T(8,128)(2,1)S(1)}, bf16[1,256,1024]{2,1,0:T(8,128)(2,1)}, u32[]{:S(2)}) copy-start(bf16[1,256,1024]{2,1,0:T(8,128)(2,1)} %param.17) | copy-start | bytes 1572868
  8.4 16.7 %copy-start.6 = (bf16[1,256,256]{2,1,0:T(8,128)(2,1)S(1)}, bf16[1,256,256]{2,1,0:T(8,128)(2,1)}, u32[]{:S(2)}) copy-start(bf16[1,256,256]{2,1,0:T(8,128)(2,1)} %param.18) | copy-start | bytes 393220
  8.4 16.7 %copy-start.7 = (bf16[1,256,256]{2,1,0:T(8,128)(2,1)S(1)}, bf16[1,256,256]{2,1,0:T(8,128)(2,1)}, u32[]{:S(2)}) copy-start(bf16[1,256,256]{2,1,0:T(8,128)(2,1)} %param.19) | copy-start | bytes 393220
  8.4 16.7 %copy-start.8 = (f32[1024]{0:T(1024)S(1)}, f32[1024]{0:T(1024)}, u32[]{:S(2)}) copy-start(f32[1024]{0:T(1024)} %param.24) | copy-start | bytes 12292
  8.4 16.7 %copy-start.9 = (f32[16]{0:T(128)S(1)}, f32[16]{0:T(128)}, u32[]{:S(2)}) copy-start(f32[16]{0:T(128)} %param.21) | copy-start | bytes 196
  8.4 16.7 %copy-start.10 = (f32[16]{0:T(128)S(1)}, f32[16]{0:T(128)}, u32[]{:S(2)}) copy-start(f32[16]{0:T(128)} %param.22) | copy-start | bytes 196
  10.4 14.3 %all-to-all-start = ((bf16[16,16,4,256]{3,2,1,0:T(4,128)(2,1)}), bf16[16,16,4,256]{3,2,1,0:T(4,128)(2,1)S(1)}, u32[]{:S(2)}, u32[]{:S(2)}) async-start(bf16[16,16,4,256]{3,2,1,0:T(4,128)(2,1)} %gather_fusion), calls=%async_computation | async-start | bytes 1048576 | tf_op jit(solution)/shard_map/all_to_all | solution.py:328
  16.9 137.1 %reduce-scatter.2.cloned.1.call-start = ((), (), s32[]{:S(2)}) async-start(), calls=%async_computation.4 | async-start | bytes 4718592 | tf_op jit(solution)/shard_map/reduce_scatter | solution.py:351
  41.9 1.9 %copy-start.1 = (bf16[256,8192]{1,0:T(8,128)(2,1)}, bf16[256,8192]{1,0:T(8,128)(2,1)S(1)}, u32[]{:S(2)}) copy-start(bf16[256,8192]{1,0:T(8,128)(2,1)S(1)} %get-tuple-element.10) | copy-start | bytes 12582916
  43.9 0.7 copy-start.11
  47.4 38.6 %copy-start.2 = (bf16[128,2,32,128]{3,2,1,0:T(8,128)(2,1)}, bf16[128,2,32,128]{3,2,1,0:T(8,128)(2,1)S(1)}, u32[]{:S(2)}) copy-start(bf16[128,2,32,128]{3,2,1,0:T(8,128)(2,1)S(1)} %get-tuple-element.12) | copy-start | bytes 6291460
  86.1 10.0 %copy-start.19 = (s32[16]{0:T(128)S(1)}, s32[16]{0:T(128)}, u32[]{:S(2)}) copy-start(s32[16]{0:T(128)} %param.30) | copy-start | bytes 196
  86.1 10.7 %copy-start.14 = (bf16[2,1,256,128]{3,2,1,0:T(8,128)(2,1)S(1)}, bf16[2,1,256,128]{3,2,1,0:T(8,128)(2,1)}, u32[]{:S(2)}) copy-start(bf16[2,1,256,128]{3,2,1,0:T(8,128)(2,1)} %param.28) | copy-start | bytes 393220
  86.1 40.5 %all-to-all-start.1 = ((bf16[128,2,32,128]{3,2,1,0:T(8,128)(2,1)}), bf16[128,2,32,128]{3,2,1,0:T(8,128)(2,1)S(1)}, u32[]{:S(2)}, u32[]{:S(2)}) async-start(bf16[128,2,32,128]{3,2,1,0:T(8,128)(2,1)} %copy-done.2), calls=%async_computation.2 | async-start | bytes 4194304 | tf_op jit(solution)/shard_map/all_to_all | solution.py:333
  96.7 1.6 copy-start.3
  98.3 1.0 copy-start.12
  125.6 1.0 copy-start.15
  126.5 1.0 copy-start.13
  127.6 1.2 copy-start.16
Sparse Core Ops, SparseCore 0:
  44.0 81.0 reduce-scatter.1

commit v2 on v1

--- a/solution.py
+++ b/solution.py
@@ -12,32 +12,36 @@
 STATE = 256
 ATT_DIM = 128
 ROWS = 64
-CHUNKS = ((0, 32), (32, 32))
-KEY_BLOCK = 1024
+CHUNKS = ((0, 48), (48, 16))
+KEY_SOURCES = 32
+AHEAD = 2
 VMEM_LIMIT = 48 * 1024 * 1024
 NEG = -1e30
 
 
 def pack_kernel(order_ref, kv_ref, *refs):
-    outs, sem = refs[:-1], refs[-1]
+    outs, (held, in_sem, out_sem) = refs[:-3], refs[-3:]
     slots = kv_ref.shape[1]
     tensor = kv_ref.shape[3] // ATT_DIM
 
-    def copies(slot):
-        taken = order_ref[slot]
+    def fetch(slot):
+        return pltpu.make_async_copy(
+            kv_ref.at[:, order_ref[slot]], held.at[slot], in_sem.at[slot]
+        )
+
+    for slot in range(slots):
+        fetch(slot).start()
+    for slot in range(slots):
+        fetch(slot).wait()
         for number, ((first, rows), out) in enumerate(zip(CHUNKS, outs)):
             for h in range(tensor):
-                yield pltpu.make_async_copy(
-                    kv_ref.at[:, taken, pl.ds(first, rows), pl.ds(h * ATT_DIM, ATT_DIM)],
+                pltpu.make_async_copy(
+                    held.at[slot, :, pl.ds(first, rows), pl.ds(h * ATT_DIM, ATT_DIM)],
                     out.at[slot * tensor + h],
-                    sem.at[number],
-                )
-
-    for slot in range(slots):
-        for copy in copies(slot):
-            copy.start()
+                    out_sem.at[number],
+                ).start()
     for number, out in enumerate(outs):
-        pltpu.make_async_copy(out, out, sem.at[number]).wait()
+        pltpu.make_async_copy(out, out, out_sem.at[number]).wait()
 
 
 def pack(order, prefix_kv):
@@ -51,7 +55,11 @@
         ],
         in_specs=[pl.BlockSpec(memory_space=pltpu.SMEM), pl.BlockSpec(memory_space=pl.ANY)],
         out_specs=[pl.BlockSpec(memory_space=pl.ANY) for _ in CHUNKS],
-        scratch_shapes=[pltpu.SemaphoreType.DMA((len(CHUNKS),))],
+        scratch_shapes=[
+            pltpu.VMEM((slots, 2) + prefix_kv.shape[2:], jnp.bfloat16),
+            pltpu.SemaphoreType.DMA((slots,)),
+            pltpu.SemaphoreType.DMA((len(CHUNKS),)),
+        ],
         compiler_params=pltpu.CompilerParams(vmem_limit_bytes=VMEM_LIMIT),
         cost_estimate=pl.CostEstimate(flops=0, bytes_accessed=8 << 20, transcendentals=0),
         name="pack_prefix",
@@ -183,19 +191,23 @@
     sources = kv_ref.shape[0]
     block = sources * rows
 
-    def scores(h, keys2):
-        return jnp.dot(keys2, qt_ref[h], preferred_element_type=f32)
-
     def update(keys, values, mask, start):
         keys2 = jnp.concatenate([keys, keys], axis=1)
         size = values.shape[0]
         ones = jnp.ones((size, 16), bf16)
         values_t = jnp.concatenate([values.T, ones.T], axis=0)
-        for h in range(heads):
-            s = scores(h, keys2)
+
+        def score(h):
+            s = jnp.dot(keys2, qt_ref[h], preferred_element_type=f32)
             if mask is not None:
                 s = jnp.where(mask, s, NEG)
-            peak = jnp.max(s, axis=0, keepdims=True)
+            return s, jnp.max(s, axis=0, keepdims=True)
+
+        ahead = [score(h) for h in range(AHEAD)]
+        for h in range(heads):
+            if h + AHEAD < heads:
+                ahead.append(score(h + AHEAD))
+            s, peak = ahead.pop(0)
             if start:
                 top = peak
             else:
@@ -264,7 +276,7 @@
     seg, width = queries.shape
     heads = width // ATT_DIM
     sources, _, rows, _ = kv.shape
-    per = KEY_BLOCK // rows
+    per = KEY_SOURCES
     first = carry is None
 
     def whole(shape):
@@ -297,7 +309,7 @@
         out_shape=[jax.ShapeDtypeStruct(s, k) for s, k in zip(outs, kinds)],
         compiler_params=pltpu.CompilerParams(vmem_limit_bytes=VMEM_LIMIT),
         cost_estimate=pl.CostEstimate(
-            flops=8 * work * ATT_DIM, bytes_accessed=4 * sources * rows * ATT_DIM, transcendentals=work
+            flops=64 * work * ATT_DIM, bytes_accessed=4 * sources * rows * ATT_DIM, transcendentals=work
         ),
         name="attend_chunk",
     )(length[None], queries, kv, *more)
@@ -328,11 +340,15 @@
     own_state = lax.all_to_all(
         state_roll[order].astype(jnp.bfloat16), "traj", split_axis=0, concat_axis=0, tiled=True
     )
-    packed = pack(order, prefix_kv)
-    received = [
-        lax.all_to_all(part, ("traj", "tensor"), split_axis=0, concat_axis=0, tiled=True)
-        for part in packed
-    ]
+    received, before = [], own_state
+    for part in pack(order, prefix_kv):
+        before, part = lax.optimization_barrier((before, part))
+        if received:
+            received[-1] = before
+        else:
+            own_state = before
+        before = lax.all_to_all(part, ("traj", "tensor"), split_axis=0, concat_axis=0, tiled=True)
+        received.append(before)
     heads = dt_in.shape[2]
     state = jnp.transpose(own_state, (1, 0, 2, 3)).reshape(heads * HEAD_DIM, STATE)
     product, final = mixer(

time: 163 us -> 120 us (0.74)
  the two profiles are of different devices: /device:TPU:27 before, /device:TPU:1 now
where the time goes in v2:
time: 120 us; the launch traced here: 118 us
  Pallas kernels  37 us (31%)
  waiting for transfers between devices  32 us (27%)
  starting transfers between devices  20.9 us (17%)
  between operations  16.2 us (14%)
  local copies, waits for them, and re-layouts  10.8 us (9%)
    all_to_all x2, waiting for transfers between devices, local(): lax.all_to_all(part, ('traj', 'tensor'), split_axis=0, concat_axis=0, til...  25.6 us
    pallas_call x1, Pallas kernels, mixer(): pl.pallas_call(mixer_kernel, grid=(total // block,), in_specs=[whole(a) f...  16.8 us
    pallas_call x2, Pallas kernels, attend(): pl.pallas_call(functools.partial(attend_kernel, first_row, rows, first, l...  16.5 us
    all_to_all x2, starting transfers between devices, local(): lax.all_to_all(part, ('traj', 'tensor'), split_axis=0, concat_axis=0, til...  13.3 us
    all_to_all x1, starting transfers between devices, local(): lax.all_to_all(state_roll[order].astype(jnp.bfloat16), 'traj', split_axis...  7.58 us
    unnamed x39, local copies, waits for them, and re-layouts  7.21 us
    all_to_all x1, waiting for transfers between devices, local(): lax.all_to_all(state_roll[order].astype(jnp.bfloat16), 'traj', split_axis...  4.41 us
    pallas_call x1, Pallas kernels, pack(): pl.pallas_call(pack_kernel, out_shape=[jax.ShapeDtypeStruct((slots * tens...  3.67 us
  transfers between devices with their start and end apart: 4, of which 4 were waited for; matrix products, arithmetic and copies ran while one was open for 2% of the time, Pallas kernels for 31%

profile of v2, /device:TPU:1, one launch (start us, length us, event | category | flops | bytes accessed | tf_op | source)
XLA Modules:
  0.0 117.7 jit_solution(14424854470956488822)
XLA Ops:
  7.2 0.7 compare_select_fusion
  7.9 0.5 copy-done
  8.4 1.9 %gather_fusion = bf16[16,16,4,256]{3,2,1,0:T(4,128)(2,1)} fusion(f32[16,16,4,256]{3,2,1,0:T(4,128)S(1)} %copy-done, s32[1024]{0:T(1024)S(1)} %pad_clamp_fusion), kind=kCustom, calls=%fused_computation | custom fusion | bytes 1048640 | tf_op jit(solution)/shard_map/gather | solution.py:341
  10.3 7.6 %all-to-all-start = ((bf16[16,16,4,256]{3,2,1,0:T(4,128)(2,1)}), bf16[16,16,4,256]{3,2,1,0:T(4,128)(2,1)S(1)}, u32[]{:S(2)}, u32[]{:S(2)}) async-start(bf16[16,16,4,256]{3,2,1,0:T(4,128)(2,1)} %gather_fusion), calls=%async_computation | async-start | bytes 1048576 | tf_op jit(solution)/shard_map/all_to_all | solution.py:340
  17.9 0.6 copy-done.8
  18.6 3.7 %pack_prefix.1 = (bf16[128,2,48,128]{3,2,1,0:T(8,128)(2,1)S(1)}, bf16[128,2,16,128]{3,2,1,0:T(8,128)(2,1)}) custom-call(s32[16]{0:T(128)S(1)} %copy-done.8, bf16[2,16,64,1024]{3,2,1,0:T(8,128)(2,1)} %kv_ref.1), custom_call_target="tpu_custom_call" | custom-call | bytes 8388608 | tf_op jit(solution)/shard_map/pack_prefix/pallas_call | solution.py:50
  22.3 1.7 %copy-done.2 = bf16[128,2,48,128]{3,2,1,0:T(8,128)(2,1)} copy-done((bf16[128,2,48,128]{3,2,1,0:T(8,128)(2,1)}, bf16[128,2,48,128]{3,2,1,0:T(8,128)(2,1)S(1)}, u32[]{:S(2)}) %copy-start.2) | copy-done | bytes 3145752
  24.0 4.4 %all-to-all-done = bf16[16,16,4,256]{3,2,1,0:T(4,128)(2,1)S(1)} async-done(((bf16[16,16,4,256]{3,2,1,0:T(4,128)(2,1)}), bf16[16,16,4,256]{3,2,1,0:T(4,128)(2,1)S(1)}, u32[]{:S(2)}, u32[]{:S(2)}) %all-to-all-start) | async-done | bytes 524320 | tf_op jit(solution)/shard_map/all_to_all | solution.py:340
  28.5 8.5 %all-to-all-start.1 = ((bf16[128,2,48,128]{3,2,1,0:T(8,128)(2,1)}), bf16[128,2,48,128]{3,2,1,0:T(8,128)(2,1)}, u32[]{:S(2)}, u32[]{:S(2)}) async-start(bf16[128,2,48,128]{3,2,1,0:T(8,128)(2,1)} %copy-done.2), calls=%async_computation.2 | async-start | bytes 6291456 | tf_op jit(solution)/shard_map/all_to_all | solution.py:350
  37.0 0.6 dynamic_slice.7
  38.9 0.1 copy.19
  39.8 0.6 dynamic_slice.8.length_ref
  40.5 0.2 copy.20
  40.7 0.1 reshape.12.state_ref
  40.9 16.8 %mamba_mixer.1 = (bf16[256,8192]{1,0:T(8,128)(2,1)S(1)}, f32[1024,256]{1,0:T(8,128)}) custom-call(bf16[256,1024]{1,0:T(8,128)(2,1)S(1)} %bitcast.17, bf16[256,1024]{1,0:T(8,128)(2,1)S(1)} %bitcast.18, bf16[256,256]{1,0:T(8,128)(2,1)S(1)} %bitcast.19, bf16[256,256]{1,0:T(8,128)(2,1)S(1)} %bitcast.20, f32[256,16]{1,0:T(8,128)S(1)} %bitcast.16, ...), custom_call_target="tpu_custom_call" | custom-call | flops 4563402752 | bytes 29360128 | tf_op jit(solution)/shard_map/mamba_mixer/pallas_call | solution.py:151
  57.7 1.9 %copy-done.1 = bf16[256,8192]{1,0:T(8,128)(2,1)} copy-done((bf16[256,8192]{1,0:T(8,128)(2,1)}, bf16[256,8192]{1,0:T(8,128)(2,1)S(1)}, u32[]{:S(2)}) %copy-start.1) | copy-done | bytes 4194328
  59.7 18.4 %all-to-all-done.1.kv_ref = bf16[128,2,48,128]{3,2,1,0:T(8,128)(2,1)} async-done(((bf16[128,2,48,128]{3,2,1,0:T(8,128)(2,1)}), bf16[128,2,48,128]{3,2,1,0:T(8,128)(2,1)}, u32[]{:S(2)}, u32[]{:S(2)}) %all-to-all-start.1) | async-done | bytes 3145760 | tf_op jit(solution)/shard_map/all_to_all | solution.py:350
  78.1 4.8 %all-to-all-start.2 = ((bf16[128,2,16,128]{3,2,1,0:T(8,128)(2,1)}), bf16[128,2,16,128]{3,2,1,0:T(8,128)(2,1)S(1)}, u32[]{:S(2)}, u32[]{:S(2)}) async-start(bf16[128,2,16,128]{3,2,1,0:T(8,128)(2,1)} %get-tuple-element.20), calls=%async_computation.3 | async-start | bytes 2097152 | tf_op jit(solution)/shard_map/all_to_all | solution.py:350
  82.9 11.1 %attend_chunk.2 = (f32[8,256]{1,0:T(8,128)S(1)}, f32[8,256]{1,0:T(8,128)S(1)}, f32[8,128,256]{2,1,0:T(8,128)S(1)}) custom-call(s32[1]{0:T(128)} %dynamic_slice.8.length_ref, bf16[256,1024]{1,0:T(8,128)(2,1)S(1)} %bitcast.24, bf16[128,2,48,128]{3,2,1,0:T(8,128)(2,1)} %all-to-all-done.1.kv_ref, bf16[2,256,128]{2,1,0:T(8,128)(2,1)S(1)} %bitcast.26), custom_call_target="tpu_custom_call" | custom-call | flops 103079215104 | bytes 3145728 | tf_op jit(solution)/shard_map/attend_chunk/pallas_call | solution.py:294
  94.0 1.0 copy-done.14
  95.0 7.2 %all-to-all-done.2.kv_ref = bf16[128,2,16,128]{3,2,1,0:T(8,128)(2,1)S(1)} async-done(((bf16[128,2,16,128]{3,2,1,0:T(8,128)(2,1)}), bf16[128,2,16,128]{3,2,1,0:T(8,128)(2,1)S(1)}, u32[]{:S(2)}, u32[]{:S(2)}) %all-to-all-start.2) | async-done | bytes 1048608 | tf_op jit(solution)/shard_map/all_to_all | solution.py:350
  102.2 1.2 %copy-done.15 = f32[8,128,256]{2,1,0:T(8,128)S(1)} copy-done((f32[8,128,256]{2,1,0:T(8,128)S(1)}, f32[8,128,256]{2,1,0:T(8,128)}, u32[]{:S(2)}) %copy-start.15) | copy-done | bytes 1048600
  103.4 5.4 %attend_chunk.3 = bf16[256,1024]{1,0:T(8,128)(2,1)} custom-call(s32[1]{0:T(128)} %dynamic_slice.8.length_ref, bf16[256,1024]{1,0:T(8,128)(2,1)S(1)} %bitcast.25, bf16[128,2,16,128]{3,2,1,0:T(8,128)(2,1)S(1)} %all-to-all-done.2.kv_ref, f32[8,256]{1,0:T(8,128)S(1)} %get-tuple-element.22.refs_0_, f32[8,256]{1,0:T(8,128)S(1)} %get-tuple-element.23.refs_1_, ...), custom_call_target="tpu_custom_call" | custom-call | flops 34359738368 | bytes 1048576 | tf_op jit(solution)/shard_map/attend_chunk/pallas_call | solution.py:294
  108.8 2.0 %reduce-scatter.2.cloned.1.call-done = bf16[1,256,1024]{2,1,0:T(8,128)(2,1)} async-done(((bf16[1,256,8192]{2,1,0:T(8,128)(2,1)}), bf16[1,256,1024]{2,1,0:T(8,128)(2,1)}) %reduce-scatter.2.cloned.1.call-update) | async-done | bytes 524304 | tf_op jit(solution)/shard_map/reduce_scatter | solution.py:367
  (37 shorter events, 0.3 us)
Async XLA Ops:
  7.2 1.2 %copy-start = (f32[16,16,4,256]{3,2,1,0:T(4,128)S(1)}, f32[16,16,4,256]{3,2,1,0:T(4,128)}, u32[]{:S(2)}) copy-start(f32[16,16,4,256]{3,2,1,0:T(4,128)} %param.26) | copy-start | bytes 3145732
  10.3 18.1 %all-to-all-start = ((bf16[16,16,4,256]{3,2,1,0:T(4,128)(2,1)}), bf16[16,16,4,256]{3,2,1,0:T(4,128)(2,1)S(1)}, u32[]{:S(2)}, u32[]{:S(2)}) async-start(bf16[16,16,4,256]{3,2,1,0:T(4,128)(2,1)} %gather_fusion), calls=%async_computation | async-start | bytes 1048576 | tf_op jit(solution)/shard_map/all_to_all | solution.py:340
  17.9 0.7 copy-start.8
  22.2 1.7 %copy-start.2 = (bf16[128,2,48,128]{3,2,1,0:T(8,128)(2,1)}, bf16[128,2,48,128]{3,2,1,0:T(8,128)(2,1)S(1)}, u32[]{:S(2)}) copy-start(bf16[128,2,48,128]{3,2,1,0:T(8,128)(2,1)S(1)} %get-tuple-element.18) | copy-start | bytes 9437188
  24.0 13.0 %copy-start.9 = (s32[16]{0:T(128)S(1)}, s32[16]{0:T(128)}, u32[]{:S(2)}) copy-start(s32[16]{0:T(128)} %order_ref.1) | copy-start | bytes 196
  24.0 14.9 %copy-start.16 = (f32[1,256,16]{1,2,0:T(8,128)S(1)}, f32[1,256,16]{1,2,0:T(8,128)}, u32[]{:S(2)}) copy-start(f32[1,256,16]{1,2,0:T(8,128)} %param.20) | copy-start | bytes 49156
  24.0 15.0 %copy-start.17 = (f32[16]{0:T(128)S(1)}, f32[16]{0:T(128)}, u32[]{:S(2)}) copy-start(f32[16]{0:T(128)} %param.23) | copy-start | bytes 196
  24.0 15.8 %copy-start.18 = (s32[16]{0:T(128)S(1)}, s32[16]{0:T(128)}, u32[]{:S(2)}) copy-start(s32[16]{0:T(128)} %param.30) | copy-start | bytes 196
  28.4 12.4 %copy-start.3 = (bf16[1,256,1024]{2,1,0:T(8,128)(2,1)S(1)}, bf16[1,256,1024]{2,1,0:T(8,128)(2,1)}, u32[]{:S(2)}) copy-start(bf16[1,256,1024]{2,1,0:T(8,128)(2,1)} %param.16) | copy-start | bytes 1572868
  28.4 12.4 %copy-start.4 = (bf16[1,256,1024]{2,1,0:T(8,128)(2,1)S(1)}, bf16[1,256,1024]{2,1,0:T(8,128)(2,1)}, u32[]{:S(2)}) copy-start(bf16[1,256,1024]{2,1,0:T(8,128)(2,1)} %param.17) | copy-start | bytes 1572868
  28.4 12.4 %copy-start.5 = (bf16[1,256,256]{2,1,0:T(8,128)(2,1)S(1)}, bf16[1,256,256]{2,1,0:T(8,128)(2,1)}, u32[]{:S(2)}) copy-start(bf16[1,256,256]{2,1,0:T(8,128)(2,1)} %param.18) | copy-start | bytes 393220
  28.4 12.4 %copy-start.6 = (bf16[1,256,256]{2,1,0:T(8,128)(2,1)S(1)}, bf16[1,256,256]{2,1,0:T(8,128)(2,1)}, u32[]{:S(2)}) copy-start(bf16[1,256,256]{2,1,0:T(8,128)(2,1)} %param.19) | copy-start | bytes 393220
  28.4 12.4 %copy-start.7 = (f32[1024]{0:T(1024)S(1)}, f32[1024]{0:T(1024)}, u32[]{:S(2)}) copy-start(f32[1024]{0:T(1024)} %param.24) | copy-start | bytes 12292
  28.4 12.4 %copy-start.10 = (f32[16]{0:T(128)S(1)}, f32[16]{0:T(128)}, u32[]{:S(2)}) copy-start(f32[16]{0:T(128)} %param.21) | copy-start | bytes 196
  28.4 12.4 %copy-start.11 = (f32[16]{0:T(128)S(1)}, f32[16]{0:T(128)}, u32[]{:S(2)}) copy-start(f32[16]{0:T(128)} %param.22) | copy-start | bytes 196
  28.5 49.6 %all-to-all-start.1 = ((bf16[128,2,48,128]{3,2,1,0:T(8,128)(2,1)}), bf16[128,2,48,128]{3,2,1,0:T(8,128)(2,1)}, u32[]{:S(2)}, u32[]{:S(2)}) async-start(bf16[128,2,48,128]{3,2,1,0:T(8,128)(2,1)} %copy-done.2), calls=%async_computation.2 | async-start | bytes 6291456 | tf_op jit(solution)/shard_map/all_to_all | solution.py:350
  37.0 73.9 %reduce-scatter.2.cloned.1.call-start = ((), (), s32[]{:S(2)}) async-start(), calls=%async_computation.4 | async-start | bytes 4718592 | tf_op jit(solution)/shard_map/reduce_scatter | solution.py:367
  57.7 1.9 %copy-start.1 = (bf16[256,8192]{1,0:T(8,128)(2,1)}, bf16[256,8192]{1,0:T(8,128)(2,1)S(1)}, u32[]{:S(2)}) copy-start(bf16[256,8192]{1,0:T(8,128)(2,1)S(1)} %get-tuple-element.16) | copy-start | bytes 12582916
  59.6 23.2 %copy-start.12 = (bf16[1,256,1024]{2,1,0:T(8,128)(2,1)S(1)}, bf16[1,256,1024]{2,1,0:T(8,128)(2,1)}, u32[]{:S(2)}) copy-start(bf16[1,256,1024]{2,1,0:T(8,128)(2,1)} %param.27) | copy-start | bytes 1572868
  59.6 23.2 %copy-start.13 = (bf16[2,1,256,128]{3,2,1,0:T(8,128)(2,1)S(1)}, bf16[2,1,256,128]{3,2,1,0:T(8,128)(2,1)}, u32[]{:S(2)}) copy-start(bf16[2,1,256,128]{3,2,1,0:T(8,128)(2,1)} %param.28) | copy-start | bytes 393220
  78.1 24.1 %all-to-all-start.2 = ((bf16[128,2,16,128]{3,2,1,0:T(8,128)(2,1)}), bf16[128,2,16,128]{3,2,1,0:T(8,128)(2,1)S(1)}, u32[]{:S(2)}, u32[]{:S(2)}) async-start(bf16[128,2,16,128]{3,2,1,0:T(8,128)(2,1)} %get-tuple-element.20), calls=%async_computation.3 | async-start | bytes 2097152 | tf_op jit(solution)/shard_map/all_to_all | solution.py:350
  94.0 1.0 copy-start.14
  102.2 1.2 %copy-start.15 = (f32[8,128,256]{2,1,0:T(8,128)S(1)}, f32[8,128,256]{2,1,0:T(8,128)}, u32[]{:S(2)}) copy-start(f32[8,128,256]{2,1,0:T(8,128)} %copy-done.14) | copy-start | bytes 3145732
Sparse Core Ops, SparseCore 0:
  59.8 50.9 reduce-scatter.1

commit v3 on v2

v3 whole, which is shorter than its diff:
```python
import functools
import math

import jax
import jax.numpy as jnp
from jax import lax
from jax.experimental import pallas as pl
from jax.experimental.pallas import tpu as pltpu
from jax.sharding import PartitionSpec as P

HEAD_DIM = 64
STATE = 256
ATT_DIM = 128
ROWS = 64
CHUNKS = ((0, 48, 32), (48, 16, 128))
VMEM_LIMIT = 56 * 1024 * 1024
AHEAD = 3
NEG = -1e30


def pack_kernel(order_ref, kv_ref, *refs):
    outs, (held, in_sem, out_sem) = refs[:-3], refs[-3:]
    slots = kv_ref.shape[1]
    tensor = kv_ref.shape[3] // ATT_DIM

    def fetch(slot):
        return pltpu.make_async_copy(
            kv_ref.at[:, order_ref[slot]], held.at[slot], in_sem.at[slot]
        )

    for slot in range(slots):
        fetch(slot).start()
    for slot in range(slots):
        fetch(slot).wait()
        for number, ((first, rows, _), out) in enumerate(zip(CHUNKS, outs)):
            for h in range(tensor):
                pltpu.make_async_copy(
                    held.at[slot, :, pl.ds(first, rows), pl.ds(h * ATT_DIM, ATT_DIM)],
                    out.at[slot * tensor + h],
                    out_sem.at[number],
                ).start()
    for number, out in enumerate(outs):
        pltpu.make_async_copy(out, out, out_sem.at[number]).wait()


def pack(order, prefix_kv):
    slots = prefix_kv.shape[1]
    tensor = prefix_kv.shape[3] // ATT_DIM
    return pl.pallas_call(
        pack_kernel,
        out_shape=[
            pltpu.HBM((slots * tensor, 2, rows, ATT_DIM), jnp.bfloat16) for _, rows, _ in CHUNKS
        ],
        in_specs=[pl.BlockSpec(memory_space=pltpu.SMEM), pl.BlockSpec(memory_space=pltpu.HBM)],
        out_specs=[pl.BlockSpec(memory_space=pltpu.HBM) for _ in CHUNKS],
        scratch_shapes=[
            pltpu.VMEM((slots, 2) + prefix_kv.shape[2:], jnp.bfloat16),
            pltpu.SemaphoreType.DMA((slots,)),
            pltpu.SemaphoreType.DMA((len(CHUNKS),)),
        ],
        compiler_params=pltpu.CompilerParams(vmem_limit_bytes=VMEM_LIMIT),
        cost_estimate=pl.CostEstimate(flops=0, bytes_accessed=8 << 20, transcendentals=0),
        name="pack_prefix",
    )(order, prefix_kv)


def mixer_kernel(
    first_ref,
    x_ref, gate_ref, b_ref, c_ref, dt_ref, bias_ref, rate_ref, skip_ref, gain_ref, state_ref, w_ref,
    out_ref, normed, final_ref, y_ref, xt_ref, w_held, w_sem,
):
    seg, width = x_ref.shape
    heads = dt_ref.shape[1]
    block = out_ref.shape[2]
    blocks = w_held.shape[0]
    f32, bf16 = jnp.float32, jnp.bfloat16
    at = pl.program_id(0)

    def fetch(i):
        span = pl.ds(pl.multiple_of((2 * i + first_ref[0]) * block, block), block)
        return pltpu.make_async_copy(w_ref.at[:, span], w_held.at[i], w_sem.at[i])

    @pl.when(at == 0)
    def _():
        for i in range(blocks):
            fetch(i).start()
        raw = dt_ref[...] + bias_ref[...]
        step = jnp.maximum(raw, 0.0) + jnp.log1p(jnp.exp(-jnp.abs(raw)))
        rows = lax.broadcasted_iota(jnp.int32, (seg, seg), 0)
        cols = lax.broadcasted_iota(jnp.int32, (seg, seg), 1)
        causal = rows >= cols
        lower = jnp.where(causal, 1.0, 0.0).astype(f32)
        pad = jnp.zeros((seg, 128 - heads), f32)
        decay = jnp.concatenate([-step * (rate_ref[...] * math.log2(math.e)), pad], axis=1)
        cum = jnp.dot(lower, decay, precision=lax.Precision.HIGHEST, preferred_element_type=f32)
        behind = cum - jnp.log2(jnp.concatenate([step, pad + 1.0], axis=1))
        behind_t = behind.T
        last = cum[seg - 1 : seg, :]
        grow = jnp.exp2(cum)
        tail = jnp.exp2(last - behind)
        c = c_ref[...]
        b = b_ref[...]
        inner = lax.dot_general(c, b, (((1,), (1,)), ((), ())), preferred_element_type=f32)
        lane = lax.broadcasted_iota(jnp.int32, (seg, 128), 1)
        first = lane < HEAD_DIM
        square = jnp.zeros((seg, 128), f32)
        for p in range(heads // 2):
            h = 2 * p
            span = pl.ds(p * 128, 128)
            x = x_ref[:, span]
            x_f = x.astype(f32)

            def mixed_with(k):
                diff = jnp.where(causal, cum[:, k : k + 1] - behind_t[k : k + 1, :], NEG)
                mix = jnp.exp2(diff) * inner
                return jnp.dot(mix.astype(bf16), x, preferred_element_type=f32)

            def spread(a):
                return jnp.where(first, a[:, h : h + 1], a[:, h + 1 : h + 2])

            carried = lax.dot_general(
                c, state_ref[span, :], (((1,), (1,)), ((), ())), preferred_element_type=f32
            )
            y = jnp.where(first, mixed_with(h), mixed_with(h + 1))
            y = y + spread(grow) * carried + skip_ref[:, span] * x_f
            gate = gate_ref[:, span].astype(f32)
            gated = y * (gate / (1.0 + jnp.exp(-gate)))
            y_ref[:, span] = gated
            square = square + gated * gated
            xt_ref[:, span] = (x_f * spread(tail)).astype(bf16)
        total = jnp.sum(square, axis=1, keepdims=True)
        factor = lax.rsqrt(total / width + 1e-05)
        normed[...] = (y_ref[...] * factor * gain_ref[...]).astype(bf16)

    @pl.when(at == pl.num_programs(0) - 1)
    def _():
        b = b_ref[...]
        raw = dt_ref[...] + bias_ref[...]
        step = jnp.maximum(raw, 0.0) + jnp.log1p(jnp.exp(-jnp.abs(raw)))
        keep = jnp.exp(-jnp.sum(step * rate_ref[...], axis=0, keepdims=True))
        added = lax.dot_general(xt_ref[...], b, (((0,), (0,)), ((), ())), preferred_element_type=f32)
        for h in range(heads):
            span = pl.ds(h * HEAD_DIM, HEAD_DIM)
            final_ref[span, :] = (
                keep[:, h : h + 1] * state_ref[span, :].astype(f32)
                + added[h * HEAD_DIM : (h + 1) * HEAD_DIM]
            )

    fetch(at).wait()
    out_ref[0] = jnp.dot(normed[...], w_held[at], preferred_element_type=f32).astype(bf16)


def project_kernel(first_ref, normed_ref, w_ref, arrived_ref, out_ref, w_held, w_sem):
    half, _, block = w_held.shape
    at = pl.program_id(0)

    def fetch(i):
        span = pl.ds(pl.multiple_of((2 * i + first_ref[0]) * block, block), block)
        return pltpu.make_async_copy(w_ref.at[:, span], w_held.at[i], w_sem.at[i])

    @pl.when(at == 0)
    def _():
        for i in range(half):
            fetch(i).start()

    fetch(at).wait()
    product = jnp.dot(normed_ref[...], w_held[at], preferred_element_type=jnp.float32)
    out_ref[0] = (product + arrived_ref[0].astype(jnp.float32)).astype(jnp.bfloat16)


def project(first, normed, weight, arrived):
    seg, width = normed.shape
    half, _, block = arrived.shape
    return pl.pallas_call(
        project_kernel,
        grid_spec=pltpu.PrefetchScalarGridSpec(
            num_scalar_prefetch=1,
            grid=(half,),
            in_specs=[
                pl.BlockSpec((seg, width), lambda i, n: (0, 0)),
                pl.BlockSpec(memory_space=pltpu.HBM),
                pl.BlockSpec((1, seg, block), lambda i, n: (i, 0, 0)),
            ],
            out_specs=pl.BlockSpec((1, seg, block), lambda i, n: (i, 0, 0)),
            scratch_shapes=[
                pltpu.VMEM((half, width, block), jnp.bfloat16),
                pltpu.SemaphoreType.DMA((half,)),
            ],
        ),
        out_shape=pltpu.HBM((half, seg, block), jnp.bfloat16),
        compiler_params=pltpu.CompilerParams(vmem_limit_bytes=VMEM_LIMIT),
        cost_estimate=pl.CostEstimate(
            flops=2 * seg * width * half * block,
            bytes_accessed=2 * width * half * block + 4 * half * seg * block,
            transcendentals=0,
        ),
        name="project_half",
    )(first, normed, weight, arrived)


def mixer(first, x, gate, b, c, dt, bias, rate, skip, gain, state, weight):
    seg, width = x.shape
    heads = dt.shape[1]
    block = 1024
    half = weight.shape[1] // block // 2

    def whole(a):
        return pl.BlockSpec(a.shape, lambda i, n: (0,) * a.ndim)

    small = (
        x, gate, b, c, dt, bias[None], rate[None], jnp.repeat(skip, HEAD_DIM)[None], gain[None], state
    )
    return pl.pallas_call(
        mixer_kernel,
        grid_spec=pltpu.PrefetchScalarGridSpec(
            num_scalar_prefetch=1,
            grid=(half,),
            in_specs=[whole(a) for a in small] + [pl.BlockSpec(memory_space=pltpu.HBM)],
            out_specs=[
                pl.BlockSpec((1, seg, block), lambda i, n: (i, 0, 0)),
                pl.BlockSpec((seg, width), lambda i, n: (0, 0)),
                pl.BlockSpec((width, STATE), lambda i, n: (0, 0)),
            ],
            scratch_shapes=[
                pltpu.VMEM((seg, width), jnp.float32),
                pltpu.VMEM((seg, width), jnp.bfloat16),
                pltpu.VMEM((half, width, block), jnp.bfloat16),
                pltpu.SemaphoreType.DMA((half,)),
            ],
        ),
        out_shape=[
            pltpu.HBM((half, seg, block), jnp.bfloat16),
            pltpu.HBM((seg, width), jnp.bfloat16),
            pltpu.HBM((width, STATE), jnp.float32),
        ],
        compiler_params=pltpu.CompilerParams(vmem_limit_bytes=VMEM_LIMIT),
        cost_estimate=pl.CostEstimate(
            flops=2 * seg * width * half * block + 4 * seg * seg * width,
            bytes_accessed=2 * width * half * block + 6 * seg * half * block,
            transcendentals=heads * seg * seg,
        ),
        name="mamba_mixer",
    )(first, *small, weight)


def update(qt_ref, top_ref, sum_ref, acc_ref, keys, values, mask, start):
    f32, bf16 = jnp.float32, jnp.bfloat16
    heads = acc_ref.shape[0]
    keys2 = jnp.concatenate([keys, keys], axis=1)
    size = values.shape[0]
    ones = jnp.ones((size, 16), bf16)
    values_t = jnp.concatenate([values.T, ones.T], axis=0)

    def score(h):
        s = jnp.dot(keys2, qt_ref[h], preferred_element_type=f32)
        if mask is not None:
            s = jnp.where(mask, s, NEG)
        return s, jnp.max(s, axis=0, keepdims=True)

    ahead = [score(h) for h in range(AHEAD)]
    for h in range(heads):
        if h + AHEAD < heads:
            ahead.append(score(h + AHEAD))
        s, peak = ahead.pop(0)
        if start:
            top = peak
        else:
            old = top_ref[h : h + 1, :]
            top = jnp.maximum(old, peak)
            scale = jnp.exp2(old - top)
        top_ref[h : h + 1, :] = top
        weights = jnp.exp2(s - top).astype(bf16)
        part = jnp.dot(values_t, weights, preferred_element_type=f32)
        if start:
            acc_ref[h] = part[:ATT_DIM]
            sum_ref[h : h + 1, :] = part[ATT_DIM : ATT_DIM + 1]
        else:
            acc_ref[h] = acc_ref[h] * scale + part[:ATT_DIM]
            sum_ref[h : h + 1, :] = (
                sum_ref[h : h + 1, :] * scale + part[ATT_DIM : ATT_DIM + 1]
            )


def attend_new_kernel(q_ref, new_ref, top_ref, sum_ref, acc_ref, qt_ref):
    f32, bf16 = jnp.float32, jnp.bfloat16
    seg = q_ref.shape[0]
    factor = math.log2(math.e) / math.sqrt(ATT_DIM)
    for h in range(qt_ref.shape[0]):
        q = q_ref[:, h * ATT_DIM : (h + 1) * ATT_DIM].astype(f32).T * factor
        high = q.astype(bf16)
        qt_ref[h, :ATT_DIM, :] = high
        qt_ref[h, ATT_DIM:, :] = (q - high.astype(f32)).astype(bf16)
    keys = lax.broadcasted_iota(jnp.int32, (seg, seg), 0)
    tokens = lax.broadcasted_iota(jnp.int32, (seg, seg), 1)
    update(
        qt_ref, top_ref, sum_ref, acc_ref, new_ref[0], new_ref[1], keys <= tokens, True
    )


def attend_new(queries, new_kv):
    seg, width = queries.shape
    heads = width // ATT_DIM
    vmem = pl.BlockSpec(memory_space=pltpu.VMEM)
    return pl.pallas_call(
        attend_new_kernel,
        in_specs=[vmem, vmem],
        out_specs=[vmem] * 4,
        out_shape=[
            pltpu.HBM((heads, seg), jnp.float32),
            pltpu.HBM((heads, seg), jnp.float32),
            pltpu.HBM((heads, ATT_DIM, seg), jnp.float32),
            pltpu.HBM((heads, 2 * ATT_DIM, seg), jnp.bfloat16),
        ],
        compiler_params=pltpu.CompilerParams(vmem_limit_bytes=VMEM_LIMIT),
        cost_estimate=pl.CostEstimate(
            flops=8 * seg * seg * width, bytes_accessed=16 * seg * width, transcendentals=seg * seg * heads
        ),
        name="attend_new",
    )(queries, new_kv)


def attend_kernel(
    first_row, rows, last, order_ref, length_ref, slot_ref, qt_ref, kv_ref, top_in, sum_in, acc_in, *refs
):
    bf16 = jnp.bfloat16
    outs, state = refs[:-3], refs[-3:]
    top_ref, sum_ref, acc_ref = state
    heads, _, seg = qt_ref.shape
    step = pl.program_id(0)
    sources = kv_ref.shape[0]
    block = sources * rows

    @pl.when(step == 0)
    def _():
        top_ref[...] = top_in[...]
        sum_ref[...] = sum_in[...]
        acc_ref[...] = acc_in[...]

    length = length_ref[order_ref[slot_ref[0]]]
    start = step * sources * ROWS + first_row
    end = start + (sources - 1) * ROWS + rows

    def block_of(which):
        return kv_ref[:, which].reshape(block, ATT_DIM)

    @pl.when(end <= length)
    def _():
        update(qt_ref, *state, block_of(0), block_of(1), None, False)

    @pl.when((start < length) & (end > length))
    def _():
        row = lax.broadcasted_iota(jnp.int32, (block, seg), 0)
        place = start + row // rows * ROWS + row % rows
        update(qt_ref, *state, block_of(0), block_of(1), place < length, False)

    @pl.when(step == pl.num_programs(0) - 1)
    def _():
        if last:
            for h in range(heads):
                result = acc_ref[h] / sum_ref[h : h + 1, :]
                outs[0][:, h * ATT_DIM : (h + 1) * ATT_DIM] = result.T.astype(bf16)
        else:
            outs[0][...] = top_ref[...]
            outs[1][...] = sum_ref[...]
            outs[2][...] = acc_ref[...]


def attend(order, prefix_len, slot, qt, kv, carry, first_row, per, last):
    heads, _, seg = qt.shape
    sources, _, rows, _ = kv.shape

    def whole(shape):
        return pl.BlockSpec(shape, lambda i, *_: (0,) * len(shape))

    qt, *carry = [pltpu.with_memory_space_constraint(a, pltpu.HBM) for a in (qt, *carry)]
    carried = [a.shape for a in carry]
    outs = [(seg, heads * ATT_DIM)] if last else carried
    kind = jnp.bfloat16 if last else jnp.float32

    def at(i, order, lengths, slot):
        length = lengths[order[slot[0]]]
        return (jnp.minimum(i, (length - 1 - first_row) // (per * ROWS)), 0, 0, 0)

    work = sources * rows * seg * heads
    result = pl.pallas_call(
        functools.partial(attend_kernel, first_row, rows, last),
        grid_spec=pltpu.PrefetchScalarGridSpec(
            num_scalar_prefetch=3,
            grid=(sources // per,),
            in_specs=[whole(qt.shape), pl.BlockSpec((per, 2, rows, ATT_DIM), at)]
            + [whole(s) for s in carried],
            out_specs=[whole(s) for s in outs],
            scratch_shapes=[pltpu.VMEM(s, jnp.float32) for s in carried],
        ),
        out_shape=[pltpu.HBM(s, kind) for s in outs],
        compiler_params=pltpu.CompilerParams(vmem_limit_bytes=(32 if last else 56) * 1024 * 1024),
        cost_estimate=pl.CostEstimate(
            flops=64 * work * ATT_DIM, bytes_accessed=4 * sources * rows * ATT_DIM, transcendentals=work
        ),
        name="attend_chunk",
    )(order, prefix_len, slot, qt, kv, *carry)
    return result[0] if last else tuple(result)


def local(
    ssm_in,
    gate_in,
    b_in,
    c_in,
    dt_in,
    dt_bias,
    decay_rate,
    skip,
    norm_gain,
    out_weight,
    state_roll,
    query,
    new_kv,
    prefix_kv,
    prefix_len,
    order,
):
    slot = lax.axis_index("traj")
    own_state = lax.all_to_all(
        state_roll.at[order]
        .get(mode="promise_in_bounds", wrap_negative_indices=False)
        .astype(jnp.bfloat16),
        "traj", split_axis=0, concat_axis=0, tiled=True
    )
    prefix_kv = pltpu.with_memory_space_constraint(prefix_kv, pltpu.HBM)
    received, ahead = [], own_state
    for part in pack(order, prefix_kv):
        ahead, part = lax.optimization_barrier((ahead, part))
        if received:
            received[-1] = ahead
        else:
            own_state = ahead
        ahead = lax.all_to_all(part, ("traj", "tensor"), split_axis=0, concat_axis=0, tiled=True)
        received.append(ahead)
    heads = dt_in.shape[2]
    state = jnp.transpose(own_state, (1, 0, 2, 3)).reshape(heads * HEAD_DIM, STATE)
    place = lax.axis_index("tensor")
    core = place % 2
    tensor = lax.axis_size("tensor")
    other, normed, final_state = mixer(
        (1 - core)[None],
        ssm_in[0],
        gate_in[0],
        b_in[0],
        c_in[0],
        dt_in[0],
        dt_bias,
        decay_rate,
        skip,
        norm_gain,
        state,
        out_weight,
    )
    arrived = lax.ppermute(other, "tensor", [(i, i ^ 1) for i in range(tensor)])
    *carry, qt = attend_new(query[0], new_kv[:, 0])
    normed, carry[0] = lax.optimization_barrier((normed, carry[0]))
    mixed = lax.psum_scatter(
        project(core[None], normed, out_weight, arrived),
        "tensor",
        scatter_dimension=0,
        tiled=True,
        axis_index_groups=[list(range(c, tensor, 2)) for c in range(2)],
    )
    for number, (part, (first_row, _, per)) in enumerate(zip(received, CHUNKS)):
        last = number == len(CHUNKS) - 1
        carry = attend(order, prefix_len, slot[None], qt, part, carry, first_row, per, last)
    return (mixed, final_state.reshape(1, heads, HEAD_DIM, STATE), carry[None])


def solution(mesh):
    in_specs = (
        P("traj", None, "tensor"),
        P("traj", None, "tensor"),
        P("traj", None, "tensor"),
        P("traj", None, "tensor"),
        P("traj", None, "tensor"),
        P("tensor"),
        P("tensor"),
        P("tensor"),
        P("tensor"),
        P("tensor", None),
        P(None, "tensor", "traj", None),
        P("traj", None, "tensor"),
        P(None, "traj", None, "tensor"),
        P(None, None, ("traj", "tensor"), None),
        P(),
        P(),
    )
    out_specs = (
        P("traj", None, "tensor"),
        P("traj", "tensor", None, None),
        P("traj", None, "tensor"),
    )
    return jax.shard_map(local, mesh=mesh, in_specs=in_specs, out_specs=out_specs, check_vma=False)
```

time: 120 us -> 118 us (0.983); the launches traced: 118 us -> 117 us
  Pallas kernels: 37 us -> 48.2 us
  waiting for transfers between devices: 32 us -> 25.8 us
  local copies, waits for them, and re-layouts: 10.8 us -> 6.44 us
  between operations: 16.2 us -> 14.1 us
  starting transfers between devices: 20.9 us -> 22.1 us
    pallas_call x4 -> x6, Pallas kernels: 37 us -> 48.2 us  [the longest x2 24.5 us: attend(): pl.pallas_call(functools.partial(attend_kernel, first_row, rows, last), g...]
    all_to_all x2, waiting for transfers between devices: 25.6 us -> 18.9 us  [local(): lax.all_to_all(part, ('traj', 'tensor'), split_axis=0, concat_axis=0, til...]
    unnamed x39 -> x13, local copies, waits for them, and re-layouts: 7.21 us -> 2.64 us
    reduce_scatter x1, waiting for transfers between devices: 1.98 us -> 0.01 us  [local(): lax.psum_scatter(project(core[None], normed, out_weight, arrived), 'tenso...]
    all_to_all x1, waiting for transfers between devices: 4.41 us -> 6.05 us  [local(): lax.all_to_all(state_roll.at[order].get(mode='promise_in_bounds', wrap_ne...]
  transfers between devices with their start and end apart: 4 -> 5, of which waited for: 4 -> 4; matrix products, arithmetic and copies ran while one was open for 2% -> 2% of each run, Pallas kernels for 31% -> 41%
where the time goes in v3:
time: 118 us; the launch traced here: 117 us
  Pallas kernels  48.2 us (41%)
  waiting for transfers between devices  25.8 us (22%)
  starting transfers between devices  22.1 us (19%)
  between operations  14.1 us (12%)
  local copies, waits for them, and re-layouts  6.44 us (5%)
    pallas_call x2, Pallas kernels, attend(): pl.pallas_call(functools.partial(attend_kernel, first_row, rows, last), g...  24.5 us
    all_to_all x2, waiting for transfers between devices, local(): lax.all_to_all(part, ('traj', 'tensor'), split_axis=0, concat_axis=0, til...  18.9 us
    all_to_all x2, starting transfers between devices, local(): lax.all_to_all(part, ('traj', 'tensor'), split_axis=0, concat_axis=0, til...  13.3 us
    pallas_call x1, Pallas kernels, mixer(): pl.pallas_call(mixer_kernel, grid_spec=pltpu.PrefetchScalarGridSpec(num_s...  8.77 us
    all_to_all x1, starting transfers between devices, local(): lax.all_to_all(state_roll.at[order].get(mode='promise_in_bounds', wrap_ne...  7.58 us
    pallas_call x1, Pallas kernels, project(): pl.pallas_call(project_kernel, grid_spec=pltpu.PrefetchScalarGridSpec(num...  7.43 us
    all_to_all x1, waiting for transfers between devices, local(): lax.all_to_all(state_roll.at[order].get(mode='promise_in_bounds', wrap_ne...  6.05 us
    pallas_call x1, Pallas kernels, pack(): pl.pallas_call(pack_kernel, out_shape=[pltpu.HBM((slots * tensor, 2, rows...  4.45 us
  transfers between devices with their start and end apart: 5, of which 4 were waited for; matrix products, arithmetic and copies ran while one was open for 2% of the time, Pallas kernels for 41%

profile of v3, /device:TPU:1, one launch (start us, length us, event | category | flops | bytes accessed | tf_op | source)
XLA Modules:
  0.0 117.5 jit_solution(252865023284810003)
XLA Ops:
  7.2 0.7 pad_clamp_fusion
  7.9 0.5 copy-done
  8.4 1.9 %gather_fusion = bf16[16,16,4,256]{3,2,1,0:T(4,128)(2,1)} fusion(f32[16,16,4,256]{3,2,1,0:T(4,128)S(1)} %copy-done, s32[1024]{0:T(1024)S(1)} %pad_clamp_fusion), kind=kCustom, calls=%fused_computation | custom fusion | bytes 1048640 | tf_op jit(solution)/shard_map/gather | solution.py:426
  10.3 7.6 %all-to-all-start = ((bf16[16,16,4,256]{3,2,1,0:T(4,128)(2,1)}), bf16[16,16,4,256]{3,2,1,0:T(4,128)(2,1)S(1)}, u32[]{:S(2)}, u32[]{:S(2)}) async-start(bf16[16,16,4,256]{3,2,1,0:T(4,128)(2,1)} %gather_fusion), calls=%async_computation | async-start | bytes 1048576 | tf_op jit(solution)/shard_map/all_to_all | solution.py:424
  17.9 4.4 %pack_prefix.1 = (bf16[128,2,48,128]{3,2,1,0:T(8,128)(2,1)}, bf16[128,2,16,128]{3,2,1,0:T(8,128)(2,1)}) custom-call(s32[16]{0:T(128)} %order_ref.5, bf16[2,16,64,1024]{3,2,1,0:T(8,128)(2,1)} %kv_ref.1), custom_call_target="tpu_custom_call" | custom-call | bytes 8388608 | tf_op jit(solution)/shard_map/pack_prefix/pallas_call | solution.py:49
  22.4 6.1 %all-to-all-done = bf16[16,16,4,256]{3,2,1,0:T(4,128)(2,1)S(1)} async-done(((bf16[16,16,4,256]{3,2,1,0:T(4,128)(2,1)}), bf16[16,16,4,256]{3,2,1,0:T(4,128)(2,1)S(1)}, u32[]{:S(2)}, u32[]{:S(2)}) %all-to-all-start) | async-done | bytes 524320 | tf_op jit(solution)/shard_map/all_to_all | solution.py:424
  28.4 8.5 %all-to-all-start.1 = ((bf16[128,2,48,128]{3,2,1,0:T(8,128)(2,1)}), bf16[128,2,48,128]{3,2,1,0:T(8,128)(2,1)}, u32[]{:S(2)}, u32[]{:S(2)}) async-start(bf16[128,2,48,128]{3,2,1,0:T(8,128)(2,1)} %get-tuple-element.29), calls=%async_computation.2 | async-start | bytes 6291456 | tf_op jit(solution)/shard_map/all_to_all | solution.py:438
  36.9 0.0 reduce-scatter.2.cloned.1.call-start
  37.0 0.1 broadcast_in_dim.32
  37.1 0.7 broadcast_in_dim_reshape.3.skip_ref
  37.7 0.8 copy.19
  38.5 0.2 copy.20
  38.7 0.9 reshape.12.state_ref
  39.6 8.8 %mamba_mixer.1 = (bf16[4,256,1024]{2,1,0:T(8,128)(2,1)}, bf16[256,1024]{1,0:T(8,128)(2,1)}, f32[1024,256]{1,0:T(8,128)}) custom-call(s32[1]{0:T(128)} %bitcast.1.first_ref, bf16[256,1024]{1,0:T(8,128)(2,1)} %bitcast.18, bf16[256,1024]{1,0:T(8,128)(2,1)} %bitcast.19, bf16[256,256]{1,0:T(8,128)(2,1)} %bitcast.20, bf16[256,256]{1,0:T(8,128)(2,1)} %bitcast.21, ...), custom_call_target="tpu_custom_call" | custom-call | flops 2415919104 | bytes 14680064 | tf_op jit(solution)/shard_map/mamba_mixer/pallas_call | solution.py:213
  48.4 1.2 %collective-permute-start = (bf16[4,256,1024]{2,1,0:T(8,128)(2,1)}, bf16[4,256,1024]{2,1,0:T(8,128)(2,1)S(1)}, u32[]{:S(2)}, u32[]{:S(2)}) collective-permute-start(bf16[4,256,1024]{2,1,0:T(8,128)(2,1)} %get-tuple-element.26), channel_id=1, source_target_pairs={{0,1},{1,0},{2,3},{3,2},{4,5},{5,4},{6,7},{7,6},{8,9},{9,8},{10,11... | collective-permute-start | bytes 6291464 | tf_op jit(solution)/shard_map/ppermute | solution.py:459
  49.6 3.1 %attend_new.1 = (f32[8,256]{1,0:T(8,128)}, f32[8,256]{1,0:T(8,128)}, f32[8,128,256]{2,1,0:T(8,128)}, bf16[8,256,256]{2,1,0:T(8,128)(2,1)}) custom-call(bf16[256,1024]{1,0:T(8,128)(2,1)} %bitcast.26, bf16[2,256,128]{2,1,0:T(8,128)(2,1)} %bitcast.27), custom_call_target="tpu_custom_call" | custom-call | flops 536870912 | bytes 4194304 | tf_op jit(solution)/shard_map/attend_new/pallas_call | solution.py:304
  52.7 0.9 collective-permute-done.arrived_ref
  53.6 1.4 %copy-done.3 = bf16[4,256,1024]{2,1,0:T(8,128)(2,1)} copy-done((bf16[4,256,1024]{2,1,0:T(8,128)(2,1)}, bf16[4,256,1024]{2,1,0:T(8,128)(2,1)S(1)}, u32[]{:S(2)}) %copy-start.3) | copy-done | bytes 2097176
  55.0 7.4 %project_half.1 = bf16[4,256,1024]{2,1,0:T(8,128)(2,1)} custom-call(s32[1]{0:T(128)} %bitcast.first_ref, bf16[256,1024]{1,0:T(8,128)(2,1)} %get-tuple-element.25.normed_ref, bf16[1024,8192]{1,0:T(8,128)(2,1)} %w_ref.3, bf16[4,256,1024]{2,1,0:T(8,128)(2,1)} %copy-done.3), custom_call_target="tpu_custom_call" | custom-call | flops 2147483648 | bytes 12582912 | tf_op jit(solution)/shard_map/project_half/pallas_call | solution.py:174
  62.5 15.6 %all-to-all-done.1.kv_ref = bf16[128,2,48,128]{3,2,1,0:T(8,128)(2,1)} async-done(((bf16[128,2,48,128]{3,2,1,0:T(8,128)(2,1)}), bf16[128,2,48,128]{3,2,1,0:T(8,128)(2,1)}, u32[]{:S(2)}, u32[]{:S(2)}) %all-to-all-start.1) | async-done | bytes 3145760 | tf_op jit(solution)/shard_map/all_to_all | solution.py:438
  78.0 4.8 %all-to-all-start.2 = ((bf16[128,2,16,128]{3,2,1,0:T(8,128)(2,1)}), bf16[128,2,16,128]{3,2,1,0:T(8,128)(2,1)S(1)}, u32[]{:S(2)}, u32[]{:S(2)}) async-start(bf16[128,2,16,128]{3,2,1,0:T(8,128)(2,1)} %get-tuple-element.31), calls=%async_computation.3 | async-start | bytes 2097152 | tf_op jit(solution)/shard_map/all_to_all | solution.py:438
  82.8 16.0 %attend_chunk.2 = (f32[8,256]{1,0:T(8,128)}, f32[8,256]{1,0:T(8,128)}, f32[8,128,256]{2,1,0:T(8,128)}) custom-call(s32[16]{0:T(128)} %order_ref.5, s32[16]{0:T(128)} %length_ref.3, s32[1]{0:T(128)} %bitcast.14.slot_ref, bf16[8,256,256]{2,1,0:T(8,128)(2,1)} %get-tuple-element.28.qt_ref, bf16[128,2,48,128]{3,2,1,0:T(8,128)(2,1)} %all-to-all-done.1.kv_ref, ...), custom_call_target="tpu_custom_call" | custom-call | flops 103079215104 | bytes 3145728 | tf_op jit(solution)/shard_map/attend_chunk/pallas_call | solution.py:385
  98.9 3.3 %all-to-all-done.2.kv_ref = bf16[128,2,16,128]{3,2,1,0:T(8,128)(2,1)S(1)} async-done(((bf16[128,2,16,128]{3,2,1,0:T(8,128)(2,1)}), bf16[128,2,16,128]{3,2,1,0:T(8,128)(2,1)S(1)}, u32[]{:S(2)}, u32[]{:S(2)}) %all-to-all-start.2) | async-done | bytes 1048608 | tf_op jit(solution)/shard_map/all_to_all | solution.py:438
  102.2 8.5 %attend_chunk.3 = bf16[256,1024]{1,0:T(8,128)(2,1)} custom-call(s32[16]{0:T(128)S(1)} %copy-done.1, s32[16]{0:T(128)S(1)} %copy-done.2, s32[1]{0:T(128)} %bitcast.14.slot_ref, bf16[8,256,256]{2,1,0:T(8,128)(2,1)} %get-tuple-element.28.qt_ref, bf16[128,2,16,128]{3,2,1,0:T(8,128)(2,1)S(1)} %all-to-all-done.2.kv_ref, f32[8,256]{1,0:T(8,128)} %get-tuple-element.36.top_in, ...), custom_call_target="tpu_custom_call" | custom-call | flops 34359738368 | bytes 1048576 | tf_op jit(solution)/shard_map/attend_chunk/pallas_call | solution.py:385
  (12 shorter events, 0.0 us)
Async XLA Ops:
  7.2 1.2 %copy-start = (f32[16,16,4,256]{3,2,1,0:T(4,128)S(1)}, f32[16,16,4,256]{3,2,1,0:T(4,128)}, u32[]{:S(2)}) copy-start(f32[16,16,4,256]{3,2,1,0:T(4,128)} %param.26) | copy-start | bytes 3145732
  10.3 18.1 %all-to-all-start = ((bf16[16,16,4,256]{3,2,1,0:T(4,128)(2,1)}), bf16[16,16,4,256]{3,2,1,0:T(4,128)(2,1)S(1)}, u32[]{:S(2)}, u32[]{:S(2)}) async-start(bf16[16,16,4,256]{3,2,1,0:T(4,128)(2,1)} %gather_fusion), calls=%async_computation | async-start | bytes 1048576 | tf_op jit(solution)/shard_map/all_to_all | solution.py:424
  28.4 8.6 %copy-start.5 = (f32[16]{0:T(128)S(1)}, f32[16]{0:T(128)}, u32[]{:S(2)}) copy-start(f32[16]{0:T(128)} %param.23) | copy-start | bytes 196
  28.4 9.3 %copy-start.4 = (f32[1,256,16]{1,2,0:T(8,128)S(1)}, f32[1,256,16]{1,2,0:T(8,128)}, u32[]{:S(2)}) copy-start(f32[1,256,16]{1,2,0:T(8,128)} %param.20) | copy-start | bytes 49156
  28.4 49.6 %all-to-all-start.1 = ((bf16[128,2,48,128]{3,2,1,0:T(8,128)(2,1)}), bf16[128,2,48,128]{3,2,1,0:T(8,128)(2,1)}, u32[]{:S(2)}, u32[]{:S(2)}) async-start(bf16[128,2,48,128]{3,2,1,0:T(8,128)(2,1)} %get-tuple-element.29), calls=%async_computation.2 | async-start | bytes 6291456 | tf_op jit(solution)/shard_map/all_to_all | solution.py:438
  36.9 73.7 %reduce-scatter.2.cloned.1.call-start = ((), (), s32[]{:S(2)}) async-start(), calls=%async_computation.4 | async-start | bytes 2621440 | tf_op jit(solution)/shard_map/reduce_scatter | solution.py:462
  48.4 5.2 %collective-permute-start = (bf16[4,256,1024]{2,1,0:T(8,128)(2,1)}, bf16[4,256,1024]{2,1,0:T(8,128)(2,1)S(1)}, u32[]{:S(2)}, u32[]{:S(2)}) collective-permute-start(bf16[4,256,1024]{2,1,0:T(8,128)(2,1)} %get-tuple-element.26), channel_id=1, source_target_pairs={{0,1},{1,0},{2,3},{3,2},{4,5},{5,4},{6,7},{7,6},{8,9},{9,8},{10,11... | collective-permute-start | bytes 6291464 | tf_op jit(solution)/shard_map/ppermute | solution.py:459
  53.6 1.4 %copy-start.3 = (bf16[4,256,1024]{2,1,0:T(8,128)(2,1)}, bf16[4,256,1024]{2,1,0:T(8,128)(2,1)S(1)}, u32[]{:S(2)}) copy-start(bf16[4,256,1024]{2,1,0:T(8,128)(2,1)S(1)} %collective-permute-done.arrived_ref) | copy-start | bytes 6291460
  78.0 24.1 %all-to-all-start.2 = ((bf16[128,2,16,128]{3,2,1,0:T(8,128)(2,1)}), bf16[128,2,16,128]{3,2,1,0:T(8,128)(2,1)S(1)}, u32[]{:S(2)}, u32[]{:S(2)}) async-start(bf16[128,2,16,128]{3,2,1,0:T(8,128)(2,1)} %get-tuple-element.31), calls=%async_computation.3 | async-start | bytes 2097152 | tf_op jit(solution)/shard_map/all_to_all | solution.py:438
  82.8 19.3 %copy-start.1 = (s32[16]{0:T(128)S(1)}, s32[16]{0:T(128)}, u32[]{:S(2)}) copy-start(s32[16]{0:T(128)} %order_ref.5) | copy-start | bytes 196
  82.8 19.3 %copy-start.2 = (s32[16]{0:T(128)S(1)}, s32[16]{0:T(128)}, u32[]{:S(2)}) copy-start(s32[16]{0:T(128)} %length_ref.3) | copy-start | bytes 196
Sparse Core Ops, SparseCore 0:
  62.6 43.8 reduce-scatter.1

commit v4 on v3

--- a/solution.py
+++ b/solution.py
@@ -243,9 +243,10 @@
     )(first, *small, weight)
 
 
-def update(qt_ref, top_ref, sum_ref, acc_ref, keys, values, mask, start):
+def update(qt_ref, top_ref, sum_ref, acc_ref, keys, values, mask, start, olds=None):
     f32, bf16 = jnp.float32, jnp.bfloat16
     heads = acc_ref.shape[0]
+    old_top, old_sum, old_acc = olds or (top_ref, sum_ref, acc_ref)
     keys2 = jnp.concatenate([keys, keys], axis=1)
     size = values.shape[0]
     ones = jnp.ones((size, 16), bf16)
@@ -265,7 +266,7 @@
         if start:
             top = peak
         else:
-            old = top_ref[h : h + 1, :]
+            old = old_top[h : h + 1, :]
             top = jnp.maximum(old, peak)
             scale = jnp.exp2(old - top)
         top_ref[h : h + 1, :] = top
@@ -275,9 +276,9 @@
             acc_ref[h] = part[:ATT_DIM]
             sum_ref[h : h + 1, :] = part[ATT_DIM : ATT_DIM + 1]
         else:
-            acc_ref[h] = acc_ref[h] * scale + part[:ATT_DIM]
+            acc_ref[h] = old_acc[h] * scale + part[:ATT_DIM]
             sum_ref[h : h + 1, :] = (
-                sum_ref[h : h + 1, :] * scale + part[ATT_DIM : ATT_DIM + 1]
+                old_sum[h : h + 1, :] * scale + part[ATT_DIM : ATT_DIM + 1]
             )
 
 
@@ -320,21 +321,25 @@
 
 
 def attend_kernel(
-    first_row, rows, last, order_ref, length_ref, slot_ref, qt_ref, kv_ref, top_in, sum_in, acc_in, *refs
+    first_row, rows, last, steps, order_ref, length_ref, slot_ref, qt_ref, kv_ref, top_in, sum_in, acc_in, *refs
 ):
     bf16 = jnp.bfloat16
-    outs, state = refs[:-3], refs[-3:]
+    outs, state = (refs[:1], refs[1:]) if last else ((), refs)
+    single = last and steps == 1
+    olds = (top_in, sum_in, acc_in) if single else None
     top_ref, sum_ref, acc_ref = state
     heads, _, seg = qt_ref.shape
     step = pl.program_id(0)
     sources = kv_ref.shape[0]
     block = sources * rows
 
-    @pl.when(step == 0)
-    def _():
-        top_ref[...] = top_in[...]
-        sum_ref[...] = sum_in[...]
-        acc_ref[...] = acc_in[...]
+    if not single:
+
+        @pl.when(step == 0)
+        def _():
+            top_ref[...] = top_in[...]
+            sum_ref[...] = sum_in[...]
+            acc_ref[...] = acc_in[...]
 
     length = length_ref[order_ref[slot_ref[0]]]
     start = step * sources * ROWS + first_row
@@ -345,24 +350,21 @@
 
     @pl.when(end <= length)
     def _():
-        update(qt_ref, *state, block_of(0), block_of(1), None, False)
+        update(qt_ref, *state, block_of(0), block_of(1), None, False, olds)
 
     @pl.when((start < length) & (end > length))
     def _():
         row = lax.broadcasted_iota(jnp.int32, (block, seg), 0)
         place = start + row // rows * ROWS + row % rows
-        update(qt_ref, *state, block_of(0), block_of(1), place < length, False)
-
-    @pl.when(step == pl.num_programs(0) - 1)
-    def _():
-        if last:
+        update(qt_ref, *state, block_of(0), block_of(1), place < length, False, olds)
+
+    if last:
+
+        @pl.when(step == pl.num_programs(0) - 1)
+        def _():
             for h in range(heads):
                 result = acc_ref[h] / sum_ref[h : h + 1, :]
                 outs[0][:, h * ATT_DIM : (h + 1) * ATT_DIM] = result.T.astype(bf16)
-        else:
-            outs[0][...] = top_ref[...]
-            outs[1][...] = sum_ref[...]
-            outs[2][...] = acc_ref[...]
 
 
 def attend(order, prefix_len, slot, qt, kv, carry, first_row, per, last):
@@ -383,14 +385,14 @@
 
     work = sources * rows * seg * heads
     result = pl.pallas_call(
-        functools.partial(attend_kernel, first_row, rows, last),
+        functools.partial(attend_kernel, first_row, rows, last, sources // per),
         grid_spec=pltpu.PrefetchScalarGridSpec(
             num_scalar_prefetch=3,
             grid=(sources // per,),
             in_specs=[whole(qt.shape), pl.BlockSpec((per, 2, rows, ATT_DIM), at)]
             + [whole(s) for s in carried],
             out_specs=[whole(s) for s in outs],
-            scratch_shapes=[pltpu.VMEM(s, jnp.float32) for s in carried],
+            scratch_shapes=[pltpu.VMEM(s, jnp.float32) for s in carried] if last else [],
         ),
         out_shape=[pltpu.HBM(s, kind) for s in outs],
         compiler_params=pltpu.CompilerParams(vmem_limit_bytes=(32 if last else 56) * 1024 * 1024),

time: 118 us -> 118 us (level)
  Pallas kernels: 48.2 us -> 51.7 us
  waiting for transfers between devices: 25.8 us -> 22.5 us
    pallas_call x2, Pallas kernels: 24.5 us -> 27.9 us  [attend(): pl.pallas_call(functools.partial(attend_kernel, first_row, rows, last, so...]
    all_to_all x2, waiting for transfers between devices: 18.9 us -> 15.6 us  [local(): lax.all_to_all(part, ('traj', 'tensor'), split_axis=0, concat_axis=0, til...]
  transfers between devices with their start and end apart: 5 -> 5, of which waited for: 4 -> 3; matrix products, arithmetic and copies ran while one was open for 2% -> 2% of each run, Pallas kernels for 41% -> 44%
where the time goes in v4:
time: 118 us
  Pallas kernels  51.7 us (44%)
  waiting for transfers between devices  22.5 us (19%)
  starting transfers between devices  22.1 us (19%)
  between operations  14.1 us (12%)
  local copies, waits for them, and re-layouts  6.44 us (5%)
    pallas_call x2, Pallas kernels, attend(): pl.pallas_call(functools.partial(attend_kernel, first_row, rows, last, so...  27.9 us
    all_to_all x2, waiting for transfers between devices, local(): lax.all_to_all(part, ('traj', 'tensor'), split_axis=0, concat_axis=0, til...  15.6 us
    all_to_all x2, starting transfers between devices, local(): lax.all_to_all(part, ('traj', 'tensor'), split_axis=0, concat_axis=0, til...  13.3 us
    pallas_call x1, Pallas kernels, mixer(): pl.pallas_call(mixer_kernel, grid_spec=pltpu.PrefetchScalarGridSpec(num_s...  8.77 us
    all_to_all x1, starting transfers between devices, local(): lax.all_to_all(state_roll.at[order].get(mode='promise_in_bounds', wrap_ne...  7.58 us
    pallas_call x1, Pallas kernels, project(): pl.pallas_call(project_kernel, grid_spec=pltpu.PrefetchScalarGridSpec(num...  7.43 us
    all_to_all x1, waiting for transfers between devices, local(): lax.all_to_all(state_roll.at[order].get(mode='promise_in_bounds', wrap_ne...  6.05 us
    pallas_call x1, Pallas kernels, pack(): pl.pallas_call(pack_kernel, out_shape=[pltpu.HBM((slots * tensor, 2, rows...  4.45 us
  transfers between devices with their start and end apart: 5, of which 3 were waited for; matrix products, arithmetic and copies ran while one was open for 2% of the time, Pallas kernels for 44%

profile of v4, /device:TPU:1, one launch (start us, length us, event | category | flops | bytes accessed | tf_op | source)
XLA Modules:
  0.0 117.6 jit_solution(4350494876630914350)
XLA Ops:
  7.2 0.7 pad_clamp_fusion
  7.9 0.5 copy-done
  8.4 1.9 %gather_fusion = bf16[16,16,4,256]{3,2,1,0:T(4,128)(2,1)} fusion(f32[16,16,4,256]{3,2,1,0:T(4,128)S(1)} %copy-done, s32[1024]{0:T(1024)S(1)} %pad_clamp_fusion), kind=kCustom, calls=%fused_computation | custom fusion | bytes 1048640 | tf_op jit(solution)/shard_map/gather | solution.py:428
  10.3 7.6 %all-to-all-start = ((bf16[16,16,4,256]{3,2,1,0:T(4,128)(2,1)}), bf16[16,16,4,256]{3,2,1,0:T(4,128)(2,1)S(1)}, u32[]{:S(2)}, u32[]{:S(2)}) async-start(bf16[16,16,4,256]{3,2,1,0:T(4,128)(2,1)} %gather_fusion), calls=%async_computation | async-start | bytes 1048576 | tf_op jit(solution)/shard_map/all_to_all | solution.py:426
  17.9 4.4 %pack_prefix.1 = (bf16[128,2,48,128]{3,2,1,0:T(8,128)(2,1)}, bf16[128,2,16,128]{3,2,1,0:T(8,128)(2,1)}) custom-call(s32[16]{0:T(128)} %order_ref.5, bf16[2,16,64,1024]{3,2,1,0:T(8,128)(2,1)} %kv_ref.1), custom_call_target="tpu_custom_call" | custom-call | bytes 8388608 | tf_op jit(solution)/shard_map/pack_prefix/pallas_call | solution.py:49
  22.4 6.1 %all-to-all-done = bf16[16,16,4,256]{3,2,1,0:T(4,128)(2,1)S(1)} async-done(((bf16[16,16,4,256]{3,2,1,0:T(4,128)(2,1)}), bf16[16,16,4,256]{3,2,1,0:T(4,128)(2,1)S(1)}, u32[]{:S(2)}, u32[]{:S(2)}) %all-to-all-start) | async-done | bytes 524320 | tf_op jit(solution)/shard_map/all_to_all | solution.py:426
  28.4 8.5 %all-to-all-start.1 = ((bf16[128,2,48,128]{3,2,1,0:T(8,128)(2,1)}), bf16[128,2,48,128]{3,2,1,0:T(8,128)(2,1)}, u32[]{:S(2)}, u32[]{:S(2)}) async-start(bf16[128,2,48,128]{3,2,1,0:T(8,128)(2,1)} %get-tuple-element.29), calls=%async_computation.2 | async-start | bytes 6291456 | tf_op jit(solution)/shard_map/all_to_all | solution.py:440
  36.9 0.0 reduce-scatter.2.cloned.1.call-start
  37.0 0.1 broadcast_in_dim.32
  37.1 0.7 broadcast_in_dim_reshape.3.skip_ref
  37.7 0.8 copy.19
  38.5 0.2 copy.20
  38.7 0.9 reshape.12.state_ref
  39.6 8.8 %mamba_mixer.1 = (bf16[4,256,1024]{2,1,0:T(8,128)(2,1)}, bf16[256,1024]{1,0:T(8,128)(2,1)}, f32[1024,256]{1,0:T(8,128)}) custom-call(s32[1]{0:T(128)} %bitcast.1.first_ref, bf16[256,1024]{1,0:T(8,128)(2,1)} %bitcast.18, bf16[256,1024]{1,0:T(8,128)(2,1)} %bitcast.19, bf16[256,256]{1,0:T(8,128)(2,1)} %bitcast.20, bf16[256,256]{1,0:T(8,128)(2,1)} %bitcast.21, ...), custom_call_target="tpu_custom_call" | custom-call | flops 2415919104 | bytes 14680064 | tf_op jit(solution)/shard_map/mamba_mixer/pallas_call | solution.py:213
  48.4 1.2 %collective-permute-start = (bf16[4,256,1024]{2,1,0:T(8,128)(2,1)}, bf16[4,256,1024]{2,1,0:T(8,128)(2,1)S(1)}, u32[]{:S(2)}, u32[]{:S(2)}) collective-permute-start(bf16[4,256,1024]{2,1,0:T(8,128)(2,1)} %get-tuple-element.26), channel_id=1, source_target_pairs={{0,1},{1,0},{2,3},{3,2},{4,5},{5,4},{6,7},{7,6},{8,9},{9,8},{10,11... | collective-permute-start | bytes 6291464 | tf_op jit(solution)/shard_map/ppermute | solution.py:461
  49.6 3.1 %attend_new.1 = (f32[8,256]{1,0:T(8,128)}, f32[8,256]{1,0:T(8,128)}, f32[8,128,256]{2,1,0:T(8,128)}, bf16[8,256,256]{2,1,0:T(8,128)(2,1)}) custom-call(bf16[256,1024]{1,0:T(8,128)(2,1)} %bitcast.26, bf16[2,256,128]{2,1,0:T(8,128)(2,1)} %bitcast.27), custom_call_target="tpu_custom_call" | custom-call | flops 536870912 | bytes 4194304 | tf_op jit(solution)/shard_map/attend_new/pallas_call | solution.py:305
  52.7 0.9 collective-permute-done.arrived_ref
  53.6 1.4 %copy-done.3 = bf16[4,256,1024]{2,1,0:T(8,128)(2,1)} copy-done((bf16[4,256,1024]{2,1,0:T(8,128)(2,1)}, bf16[4,256,1024]{2,1,0:T(8,128)(2,1)S(1)}, u32[]{:S(2)}) %copy-start.3) | copy-done | bytes 2097176
  55.0 7.4 %project_half.1 = bf16[4,256,1024]{2,1,0:T(8,128)(2,1)} custom-call(s32[1]{0:T(128)} %bitcast.first_ref, bf16[256,1024]{1,0:T(8,128)(2,1)} %get-tuple-element.25.normed_ref, bf16[1024,8192]{1,0:T(8,128)(2,1)} %w_ref.3, bf16[4,256,1024]{2,1,0:T(8,128)(2,1)} %copy-done.3), custom_call_target="tpu_custom_call" | custom-call | flops 2147483648 | bytes 12582912 | tf_op jit(solution)/shard_map/project_half/pallas_call | solution.py:174
  62.4 0.0 reduce-scatter.2.cloned.1.call-update
  62.5 15.6 %all-to-all-done.1.kv_ref = bf16[128,2,48,128]{3,2,1,0:T(8,128)(2,1)} async-done(((bf16[128,2,48,128]{3,2,1,0:T(8,128)(2,1)}), bf16[128,2,48,128]{3,2,1,0:T(8,128)(2,1)}, u32[]{:S(2)}, u32[]{:S(2)}) %all-to-all-start.1) | async-done | bytes 3145760 | tf_op jit(solution)/shard_map/all_to_all | solution.py:440
  78.0 4.8 %all-to-all-start.2 = ((bf16[128,2,16,128]{3,2,1,0:T(8,128)(2,1)}), bf16[128,2,16,128]{3,2,1,0:T(8,128)(2,1)S(1)}, u32[]{:S(2)}, u32[]{:S(2)}) async-start(bf16[128,2,16,128]{3,2,1,0:T(8,128)(2,1)} %get-tuple-element.31), calls=%async_computation.3 | async-start | bytes 2097152 | tf_op jit(solution)/shard_map/all_to_all | solution.py:440
  82.8 19.8 %attend_chunk.2 = (f32[8,256]{1,0:T(8,128)}, f32[8,256]{1,0:T(8,128)}, f32[8,128,256]{2,1,0:T(8,128)}) custom-call(s32[16]{0:T(128)} %order_ref.5, s32[16]{0:T(128)} %length_ref.3, s32[1]{0:T(128)} %bitcast.14.slot_ref, bf16[8,256,256]{2,1,0:T(8,128)(2,1)} %get-tuple-element.28.qt_ref, bf16[128,2,48,128]{3,2,1,0:T(8,128)(2,1)} %all-to-all-done.1.kv_ref, ...), custom_call_target="tpu_custom_call" | custom-call | flops 103079215104 | bytes 3145728 | tf_op jit(solution)/shard_map/attend_chunk/pallas_call | solution.py:387
  102.7 8.1 %attend_chunk.3 = bf16[256,1024]{1,0:T(8,128)(2,1)} custom-call(s32[16]{0:T(128)S(1)} %copy-done.1, s32[16]{0:T(128)S(1)} %copy-done.2, s32[1]{0:T(128)} %bitcast.14.slot_ref, bf16[8,256,256]{2,1,0:T(8,128)(2,1)} %get-tuple-element.28.qt_ref, bf16[128,2,16,128]{3,2,1,0:T(8,128)(2,1)S(1)} %all-to-all-done.2.kv_ref, f32[8,256]{1,0:T(8,128)} %get-tuple-element.36.top_in, ...), custom_call_target="tpu_custom_call" | custom-call | flops 34359738368 | bytes 1048576 | tf_op jit(solution)/shard_map/attend_chunk/pallas_call | solution.py:387
  (12 shorter events, 0.0 us)
Async XLA Ops:
  7.2 1.2 %copy-start = (f32[16,16,4,256]{3,2,1,0:T(4,128)S(1)}, f32[16,16,4,256]{3,2,1,0:T(4,128)}, u32[]{:S(2)}) copy-start(f32[16,16,4,256]{3,2,1,0:T(4,128)} %param.26) | copy-start | bytes 3145732
  10.3 18.1 %all-to-all-start = ((bf16[16,16,4,256]{3,2,1,0:T(4,128)(2,1)}), bf16[16,16,4,256]{3,2,1,0:T(4,128)(2,1)S(1)}, u32[]{:S(2)}, u32[]{:S(2)}) async-start(bf16[16,16,4,256]{3,2,1,0:T(4,128)(2,1)} %gather_fusion), calls=%async_computation | async-start | bytes 1048576 | tf_op jit(solution)/shard_map/all_to_all | solution.py:426
  28.4 8.6 %copy-start.5 = (f32[16]{0:T(128)S(1)}, f32[16]{0:T(128)}, u32[]{:S(2)}) copy-start(f32[16]{0:T(128)} %param.23) | copy-start | bytes 196
  28.4 9.3 %copy-start.4 = (f32[1,256,16]{1,2,0:T(8,128)S(1)}, f32[1,256,16]{1,2,0:T(8,128)}, u32[]{:S(2)}) copy-start(f32[1,256,16]{1,2,0:T(8,128)} %param.20) | copy-start | bytes 49156
  28.4 49.6 %all-to-all-start.1 = ((bf16[128,2,48,128]{3,2,1,0:T(8,128)(2,1)}), bf16[128,2,48,128]{3,2,1,0:T(8,128)(2,1)}, u32[]{:S(2)}, u32[]{:S(2)}) async-start(bf16[128,2,48,128]{3,2,1,0:T(8,128)(2,1)} %get-tuple-element.29), calls=%async_computation.2 | async-start | bytes 6291456 | tf_op jit(solution)/shard_map/all_to_all | solution.py:440
  36.9 73.9 %reduce-scatter.2.cloned.1.call-start = ((), (), s32[]{:S(2)}) async-start(), calls=%async_computation.4 | async-start | bytes 2621440 | tf_op jit(solution)/shard_map/reduce_scatter | solution.py:464
  48.4 5.2 %collective-permute-start = (bf16[4,256,1024]{2,1,0:T(8,128)(2,1)}, bf16[4,256,1024]{2,1,0:T(8,128)(2,1)S(1)}, u32[]{:S(2)}, u32[]{:S(2)}) collective-permute-start(bf16[4,256,1024]{2,1,0:T(8,128)(2,1)} %get-tuple-element.26), channel_id=1, source_target_pairs={{0,1},{1,0},{2,3},{3,2},{4,5},{5,4},{6,7},{7,6},{8,9},{9,8},{10,11... | collective-permute-start | bytes 6291464 | tf_op jit(solution)/shard_map/ppermute | solution.py:461
  53.6 1.4 %copy-start.3 = (bf16[4,256,1024]{2,1,0:T(8,128)(2,1)}, bf16[4,256,1024]{2,1,0:T(8,128)(2,1)S(1)}, u32[]{:S(2)}) copy-start(bf16[4,256,1024]{2,1,0:T(8,128)(2,1)S(1)} %collective-permute-done.arrived_ref) | copy-start | bytes 6291460
  78.0 24.6 %all-to-all-start.2 = ((bf16[128,2,16,128]{3,2,1,0:T(8,128)(2,1)}), bf16[128,2,16,128]{3,2,1,0:T(8,128)(2,1)S(1)}, u32[]{:S(2)}, u32[]{:S(2)}) async-start(bf16[128,2,16,128]{3,2,1,0:T(8,128)(2,1)} %get-tuple-element.31), calls=%async_computation.3 | async-start | bytes 2097152 | tf_op jit(solution)/shard_map/all_to_all | solution.py:440
  82.8 19.8 %copy-start.1 = (s32[16]{0:T(128)S(1)}, s32[16]{0:T(128)}, u32[]{:S(2)}) copy-start(s32[16]{0:T(128)} %order_ref.5) | copy-start | bytes 196
  82.8 19.8 %copy-start.2 = (s32[16]{0:T(128)S(1)}, s32[16]{0:T(128)}, u32[]{:S(2)}) copy-start(s32[16]{0:T(128)} %length_ref.3) | copy-start | bytes 196
Sparse Core Ops, SparseCore 0:
  62.6 43.8 reduce-scatter.1
